TPU v7x, 32 devices: a whole 2x2x4 slice. The times are simulated.
32 devices in a mesh: rep: 4 (over x, core), exp: 8 (over z, y).
Axes of the slice: x: 2, y: 2, z: 4, core: 2. Of those that a mesh axis runs over, the one named last changes fastest.
Arguments:
- trainer_weight: bfloat16 [64, 128, 7168], P('exp', None, 'rep'), may hold values from -0.125 to 0.125
- dirty: int32 [64], replicated, may hold values from 0 to 1, as said below
- rollout_owner: int32 [64], replicated, may hold values from 0 to 7, as said below
- rollout_slot: int32 [64], replicated, may hold values from 0 to 7, as said below
Outputs:
- update_tiles: bfloat16 [48, 128, 7168], P('exp')
- update_scales: bfloat16 [48, 1, 56], P('exp')
Inputs may be any that keep to these rules, and one draw needn't show every extreme that they name: At most 6 dirty experts share a rollout owner, and exactly 6 do at one owner or more. `rollout_owner`: every rollout owner holds exactly 8 experts, and no two experts e, f with e // 8 == f // 8 share a rollout owner. `rollout_slot`: the 8 experts of one rollout owner have different slots.
All inputs are finite; a program needn't handle non-finite values.
Results may differ from a plain program's by a relative error of at most 0.0011.
Values may be sent and summed in bfloat16 or wider, within the bound.
No kernel may reach another device: no remote copies, remote signals or barrier semaphores. Data moves between devices by JAX's collectives and lax.ppermute only.
A program may use at most 128 MiB of HBM per device.

v0:
```python
import jax
import jax.numpy as jnp
from jax import lax
from jax.sharding import PartitionSpec as P

B = 128
CAP = 6


def quantize(weights):
    count, rows, cols = weights.shape
    blocks = weights.astype(jnp.float32).reshape(count, rows // B, B, cols // B, B)
    largest = jnp.max(jnp.abs(blocks), axis=(2, 4))
    scale = (largest + 1e-06).astype(jnp.bfloat16)
    divisor = lax.optimization_barrier(scale).astype(jnp.float32)
    scaled = (blocks / divisor[:, :, None, :, None]).reshape(count, rows, cols).astype(jnp.bfloat16)
    return (scaled, scale)


def on_device(trainer_weight, dirty, rollout_owner, rollout_slot):
    owners = lax.axis_size("exp")
    here = lax.axis_index("exp")
    local_count = trainer_weight.shape[0]
    experts = dirty.shape[0]
    live = dirty == 1
    earlier = (
        (rollout_owner[:, None] == rollout_owner[None, :])
        & live[None, :]
        & (rollout_slot[None, :] < rollout_slot[:, None])
    )
    rank = jnp.sum(earlier.astype(jnp.int32), axis=1)
    start = here * local_count
    local_owner = lax.dynamic_slice_in_dim(rollout_owner, start, local_count)
    local_live = lax.dynamic_slice_in_dim(live, start, local_count)
    peers = jnp.arange(owners, dtype=jnp.int32)
    outgoing = ((local_owner[None, :] == peers[:, None]) & local_live[None, :]).astype(jnp.bfloat16)
    slots = jnp.arange(CAP, dtype=jnp.int32)
    wanted = (
        live[None, :] & (rollout_owner[None, :] == here) & (rank[None, :] == slots[:, None])
    ).astype(jnp.float32)
    source = (
        jnp.arange(experts, dtype=jnp.int32)[:, None] // local_count == peers[None, :]
    ).astype(jnp.float32)
    pick = jnp.dot(
        wanted, source, precision=lax.Precision.HIGHEST, preferred_element_type=jnp.float32
    )
    pick_low = pick.astype(jnp.bfloat16)
    scaled, scale = quantize(trainer_weight)
    send_tiles = jnp.einsum(
        "pj,jsd->psd", outgoing, scaled, preferred_element_type=jnp.float32
    ).astype(jnp.bfloat16)
    send_scales = jnp.einsum(
        "pj,jab->pab", outgoing, scale, preferred_element_type=jnp.float32
    ).astype(jnp.bfloat16)
    got_tiles, got_scales = (
        lax.all_to_all(send_tiles, "exp", split_axis=0, concat_axis=0, tiled=True),
        lax.all_to_all(send_scales, "exp", split_axis=0, concat_axis=0, tiled=True),
    )
    tiles = jnp.einsum(
        "cp,psd->csd", pick_low, got_tiles, preferred_element_type=jnp.float32
    ).astype(jnp.bfloat16)
    scales = jnp.einsum(
        "cp,pab->cab", pick_low, got_scales, preferred_element_type=jnp.float32
    ).astype(jnp.bfloat16)
    update_tiles, update_scales = (
        lax.all_gather(tiles, "rep", axis=2, tiled=True),
        lax.all_gather(scales, "rep", axis=2, tiled=True),
    )
    return (update_tiles, update_scales)


def solution(mesh):
    in_specs = (P("exp", None, "rep"), P(), P(), P())
    out_specs = (P("exp", None, None), P("exp", None, None))
    return jax.shard_map(
        on_device, mesh=mesh, in_specs=in_specs, out_specs=out_specs, check_vma=False
    )
```

profile of v0, /device:TPU:0, one launch (start us, length us, event | category | flops | bytes accessed | tf_op | source)
XLA Modules:
  0.0 226.6 jit_solution(15504293370222087335)
XLA Ops:
  7.2 0.7 dynamic_slice.6
  7.9 0.7 compare_and_fusion
  8.6 0.1 dynamic_slice.7
  8.7 2.7 %fusion = f32[8,1792]{1,0:T(8,128)S(1)} fusion(bf16[8,128,1792]{2,1,0:T(8,128)(2,1)} %param.4), kind=kLoop, calls=%fused_computation.2 | loop fusion | flops 5490688 | bytes 3727360 | tf_op jit(solution)/shard_map/reduce_max | solution.py:13
  11.3 0.1 bitcast_reduce_fusion
  11.4 0.1 copy.25
  11.5 0.1 copy.26
  11.6 0.1 broadcast_bitcast_fusion
  11.7 2.7 %fusion.1 = bf16[8,128,1792]{2,1,0:T(8,128)(2,1)S(1)} fusion(bf16[8,128,1792]{2,1,0:T(8,128)(2,1)} %param.4, f32[8,1792]{1,0:T(8,128)S(1)} %broadcast_bitcast_fusion), kind=kLoop, calls=%fused_computation.3 | loop fusion | flops 5505024 | bytes 7397376 | tf_op jit(solution)/shard_map/convert_element_type | solution.py:16
  14.4 2.4 %convolution_convert_fusion.1 = bf16[8,128,1792]{2,0,1:T(8,128)(2,1)S(1)} fusion(bf16[8,128,1792]{2,1,0:T(8,128)(2,1)S(1)} %fusion.1, s32[8]{0:T(128)S(1)} %dynamic_slice.6, pred[8]{0:T(512)(128)(4,1)S(1)} %dynamic_slice.7), kind=kOutput, calls=%fused_computation.5 | convolution fusion | flops 31195264 | bytes 7340072 | tf_op jit(solution)/shard_map/pj,jsd->psd/dot_general | solution.py:49
  16.8 2.5 %copy.28 = bf16[8,128,1792]{2,1,0:T(8,128)(2,1)} copy(bf16[8,128,1792]{2,0,1:T(8,128)(2,1)S(1)} %convolution_convert_fusion.1) | data formatting | bytes 7340032 | tf_op jit(solution)/shard_map/convert_element_type | solution.py:51
  19.3 0.0 copy-start
  19.3 0.0 copy-start.1
  19.3 7.4 %all-to-all-start = ((bf16[8,128,1792]{2,1,0:T(8,128)(2,1)}), bf16[8,128,1792]{2,1,0:T(8,128)(2,1)}, u32[]{:S(2)}, u32[]{:S(2)}) async-start(bf16[8,128,1792]{2,1,0:T(8,128)(2,1)} %copy.28), calls=%async_computation | async-start | bytes 7340032 | tf_op jit(solution)/shard_map/all_to_all | solution.py:56
  26.8 0.0 all-gather.4.cloned.1.call-start
  26.8 0.0 copy-done
  26.8 0.0 copy-done.1
  26.8 0.2 convert_reduce_fusion
  27.0 0.2 convolution_convert_fusion.4
  27.2 81.6 %all-to-all-done = bf16[8,128,1792]{2,1,0:T(8,128)(2,1)} async-done(((bf16[8,128,1792]{2,1,0:T(8,128)(2,1)}), bf16[8,128,1792]{2,1,0:T(8,128)(2,1)}, u32[]{:S(2)}, u32[]{:S(2)}) %all-to-all-start) | async-done | bytes 3670048 | tf_op jit(solution)/shard_map/all_to_all | solution.py:56
  108.8 6.3 %convolution_convert_fusion = bf16[6,128,1792]{2,0,1:T(8,128)(2,1)} fusion(bf16[8,128,1792]{2,1,0:T(8,128)(2,1)} %all-to-all-done, bf16[6,8]{1,0:T(8,128)(2,1)S(1)} %convolution_convert_fusion.4), kind=kOutput, calls=%fused_computation.4 | convolution fusion | flops 23396352 | bytes 6422624 | tf_op jit(solution)/shard_map/cp,psd->csd/dot_general | solution.py:59
  115.1 0.0 all-gather.4.cloned.1.call-update
  115.1 0.1 fusion.5
  115.2 9.9 %all_to_all.10 = bf16[8,1,14]{2,1,0:T(2,128)(2,1)S(1)} all-to-all(bf16[8,1,14]{2,1,0:T(2,128)(2,1)S(1)} %copy.30), channel_id=1, replica_groups=mesh['rep'=4,'exp'=8] {'exp'}, dimensions={0} | all-to-all | bytes 448 | tf_op jit(solution)/shard_map/all_to_all | solution.py:57
  125.1 0.1 fusion.4
  125.2 5.2 %all-gather.1 = bf16[4,14,6]{1,2,0:T(8,128)(2,1)S(1)} all-gather(bf16[1,14,6]{1,2,0:T(8,128)(2,1)S(1)} %fusion.4), channel_id=2, replica_groups=mesh['rep'=4,'exp'=8] {'rep'}, dimensions={0}, use_global_device_ids=true | all-gather | bytes 840 | tf_op jit(solution)/shard_map/all_gather | solution.py:67
  130.4 0.7 reshape.96
  131.1 77.3 %all-gather.4.cloned.1.call-done = bf16[6,128,7168]{2,0,1:T(8,128)(2,1)} async-done(((bf16[6,128,1792]{2,0,1:T(8,128)(2,1)}), bf16[6,128,7168]{2,0,1:T(8,128)(2,1)}) %all-gather.4.cloned.1.call-update) | async-done | bytes 11010064 | tf_op jit(solution)/shard_map/all_gather | solution.py:66
  208.4 11.3 %copy.32 = bf16[6,128,7168]{2,1,0:T(8,128)(2,1)} copy(bf16[6,128,7168]{2,0,1:T(8,128)(2,1)} %all-gather.4.cloned.1.call-done) | data formatting | bytes 22020096
  (5 shorter events, 0.0 us)
Async XLA Ops:
  19.3 7.5 %copy-start = (s32[64]{0:T(128)S(1)}, s32[64]{0:T(128)}, u32[]{:S(2)}) copy-start(s32[64]{0:T(128)} %param.6) | copy-start | bytes 772
  19.3 7.5 %copy-start.1 = (s32[64]{0:T(128)S(1)}, s32[64]{0:T(128)}, u32[]{:S(2)}) copy-start(s32[64]{0:T(128)} %param.7) | copy-start | bytes 772
  19.3 89.5 %all-to-all-start = ((bf16[8,128,1792]{2,1,0:T(8,128)(2,1)}), bf16[8,128,1792]{2,1,0:T(8,128)(2,1)}, u32[]{:S(2)}, u32[]{:S(2)}) async-start(bf16[8,128,1792]{2,1,0:T(8,128)(2,1)} %copy.28), calls=%async_computation | async-start | bytes 7340032 | tf_op jit(solution)/shard_map/all_to_all | solution.py:56
  26.8 181.6 %all-gather.4.cloned.1.call-start = ((), (), s32[]{:S(2)}) async-start(), calls=%async_computation.2 | async-start | bytes 18350080 | tf_op jit(solution)/shard_map/all_gather | solution.py:66
Sparse Core Ops, SparseCore 0:
  115.2 93.0 all-gather.3
where the time goes:
time: 227 us
  waiting for transfers between devices  159 us (70%)
  local copies, waits for them, and re-layouts  15.6 us (7%)
  blocking collectives  15.1 us (7%)
  between operations  14.1 us (6%)
  matrix products  9.11 us (4%)
  starting transfers between devices  7.45 us (3%)
  other arithmetic  6.35 us (3%)
    all_to_all x1, waiting for transfers between devices, on_device(): lax.all_to_all(send_tiles, 'exp', split_axis=0, concat_axis=0, tiled=True)  81.6 us
    all_gather x1, waiting for transfers between devices, on_device(): lax.all_gather(tiles, 'rep', axis=2, tiled=True)  77.3 us
    unnamed x6, local copies, waits for them, and re-layouts  12 us
    all_to_all x1, blocking collectives, on_device(): lax.all_to_all(send_scales, 'exp', split_axis=0, concat_axis=0, tiled=True)  9.89 us
    all_to_all x1, starting transfers between devices, on_device(): lax.all_to_all(send_tiles, 'exp', split_axis=0, concat_axis=0, tiled=True)  7.41 us
    dot_general x1, matrix products, on_device(): jnp.einsum('cp,psd->csd', pick_low, got_tiles, preferred_element_type=jnp...  6.27 us
    all_gather x1, blocking collectives, on_device(): lax.all_gather(scales, 'rep', axis=2, tiled=True)  5.16 us
  transfers between devices with their start and end apart: 2, of which 2 were waited for; matrix products, arithmetic and copies ran while one was open for 1% of the time, Pallas kernels for 0%

commit v1 on v0

--- a/solution.py
+++ b/solution.py
@@ -1,10 +1,250 @@
+import functools
+
 import jax
 import jax.numpy as jnp
 from jax import lax
+from jax.experimental import pallas as pl
+from jax.experimental.pallas import tpu as pltpu
 from jax.sharding import PartitionSpec as P
 
 B = 128
 CAP = 6
+
+ORDER = (0, 1, 2, 3, 4, 5, 6, 7)
+LIMIT = (3, 4, 5, 6, 7, 8)
+GROUPS = ((0, 1, 2), (3, 4), (5,))
+PICK, ROW, LIVE = 0, 8, 16
+VMEM_LIMIT = 8 * 1024 * 1024
+PLACE_LIMIT = 24 * 1024 * 1024
+
+ANY = pl.BlockSpec(memory_space=pl.ANY)
+HBM = pl.BlockSpec(memory_space=pltpu.HBM)
+VMEM = pl.BlockSpec(memory_space=pltpu.VMEM)
+SMEM = pl.BlockSpec(memory_space=pltpu.SMEM)
+
+
+def expert_for(owner_ref, source, dest, local_count):
+    found = jnp.int32(0)
+    for j in range(local_count):
+        at = source * local_count + j
+        found = jnp.where(owner_ref[at] == dest, at, found)
+    return found
+
+
+def pick_kernel(shifts, local_count, owner_ref, w_ref, *refs):
+    outs, sems = refs[:-1], refs[-1]
+    here = lax.axis_index("exp")
+    copies = []
+    for i, shift in enumerate(shifts):
+        local = expert_for(owner_ref, here, here ^ shift, local_count) - here * local_count
+        copies.append(pltpu.make_async_copy(w_ref.at[local], outs[i], sems.at[i]))
+        copies[-1].start()
+    for copy in copies:
+        copy.wait()
+
+
+def pick(owner, weight, shifts):
+    local_count, rows, cols = weight.shape
+    return pl.pallas_call(
+        functools.partial(pick_kernel, shifts, local_count),
+        out_shape=[jax.ShapeDtypeStruct((rows, cols), weight.dtype)] * len(shifts),
+        in_specs=[SMEM, HBM],
+        out_specs=[VMEM] * len(shifts),
+        scratch_shapes=[pltpu.SemaphoreType.DMA((len(shifts),))],
+        compiler_params=pltpu.CompilerParams(vmem_limit_bytes=VMEM_LIMIT),
+        name="pick",
+    )(owner, weight)
+
+
+def table_kernel(local_count, owner_ref, dirty_ref, slot_ref, out_ref):
+    here = lax.axis_index("exp")
+    live, slot = [], []
+    for shift in ORDER:
+        expert = expert_for(owner_ref, here ^ shift, here, local_count)
+        live.append((dirty_ref[expert] == 1).astype(jnp.int32))
+        slot.append(slot_ref[expert])
+    rank = [
+        sum(live[k] * (slot[k] < slot[m]).astype(jnp.int32) for k in range(len(ORDER)) if k != m)
+        for m in range(len(ORDER))
+    ]
+    spare, left = sum(live), list(live)
+    for j, limit in enumerate(LIMIT):
+        found, pick, row = jnp.int32(0), jnp.int32(0), spare
+        for m in range(limit):
+            take = left[m] * (1 - found)
+            pick = jnp.where(take == 1, m, pick)
+            row = jnp.where(take == 1, rank[m], row)
+            left[m] = left[m] - take
+            found = found + take
+        spare = spare + 1 - found
+        out_ref[PICK + j] = pick
+        out_ref[ROW + j] = row
+        out_ref[LIVE + j] = found
+
+
+def routing_table(owner, dirty, slot, local_count):
+    return pl.pallas_call(
+        functools.partial(table_kernel, local_count),
+        out_shape=jax.ShapeDtypeStruct((24,), jnp.int32),
+        in_specs=[SMEM] * 3,
+        out_specs=SMEM,
+        compiler_params=pltpu.CompilerParams(vmem_limit_bytes=VMEM_LIMIT),
+        name="routing_table",
+    )(owner, dirty, slot)
+
+
+def pack_kernel(j, count, table_ref, *refs):
+    out_ref, sem = refs[-2:]
+    for m in range(count):
+
+        @pl.when(table_ref[PICK + j] == m)
+        def _():
+            pltpu.make_async_copy(refs[m], out_ref, sem).start()
+
+    pltpu.make_async_copy(out_ref, out_ref, sem).wait()
+
+
+def pack(table, arrived, j, tokens):
+    return pl.pallas_call(
+        functools.partial(pack_kernel, j, len(arrived)),
+        out_shape=jax.ShapeDtypeStruct(arrived[0].shape, arrived[0].dtype),
+        in_specs=[SMEM] + [ANY] * (len(arrived) + len(tokens)),
+        out_specs=VMEM,
+        scratch_shapes=[pltpu.SemaphoreType.DMA],
+        compiler_params=pltpu.CompilerParams(vmem_limit_bytes=VMEM_LIMIT),
+        name="pack",
+    )(table, *arrived, *tokens)
+
+
+def place_kernel(spots, fresh, table_ref, *refs):
+    arrays, refs = refs[: len(spots)], refs[len(spots) :]
+    if not fresh:
+        acc_in, refs = refs[1], refs[2:]
+    out_ref, acc_out, acc_ref, held, sems = refs
+    rows, cols = arrays[0].shape
+    here = lax.axis_index("rep")
+    line = lax.broadcasted_iota(jnp.int32, acc_ref.shape, 0)
+    lane = lax.broadcasted_iota(jnp.int32, acc_ref.shape, 1)
+    acc_ref[...] = jnp.zeros_like(acc_ref) if fresh else acc_in[...]
+    copies = []
+    for i, (j, flip) in enumerate(spots):
+        first = pl.multiple_of((here ^ flip) * cols, B)
+        first_block = (here ^ flip) * (cols // B)
+        row = table_ref[ROW + j]
+        live = table_ref[LIVE + j] == 1
+        at = i * cols
+
+        @pl.when(live)
+        def _():
+            acc = acc_ref[...]
+            for c in range(0, cols, B):
+                x = arrays[i][:, c : c + B]
+                most = jnp.max(jnp.abs(x), axis=0, keepdims=True).astype(jnp.float32)
+                most = jnp.max(most, axis=1, keepdims=True)
+                scale = (most + 1e-06).astype(jnp.bfloat16).astype(jnp.float32)
+                scaled = x.astype(jnp.float32) * (1.0 / scale)
+                held[:, at + c : at + c + B] = scaled.astype(jnp.bfloat16)
+                acc = jnp.where((line == row) & (lane == first_block + c // B), scale, acc)
+            acc_ref[...] = acc
+
+        @pl.when(jnp.logical_not(live))
+        def _():
+            held[:, at : at + cols] = jnp.zeros((rows, cols), jnp.bfloat16)
+
+        copies.append(
+            pltpu.make_async_copy(
+                held.at[:, pl.ds(at, cols)], out_ref.at[row, :, pl.ds(first, cols)], sems.at[i]
+            )
+        )
+        copies[-1].start()
+
+    acc = acc_ref[...]
+    acc_out[...] = acc[: acc_out.shape[0], : acc_out.shape[1]].astype(acc_out.dtype)
+    for copy in copies:
+        copy.wait()
+
+
+def place(state, table, arrays, spots, replicas, final):
+    rows, cols = arrays[0].shape
+    fresh = state is None
+    kept = jax.ShapeDtypeStruct((8, 128), jnp.float32)
+    scales = jax.ShapeDtypeStruct((CAP, cols * replicas // B), jnp.bfloat16)
+    return pl.pallas_call(
+        functools.partial(place_kernel, spots, fresh),
+        out_shape=[
+            jax.ShapeDtypeStruct((CAP, rows, cols * replicas), jnp.bfloat16),
+            scales if final else kept,
+        ],
+        in_specs=[SMEM] + [VMEM] * len(arrays) + ([] if fresh else [HBM, VMEM]),
+        out_specs=[HBM, VMEM],
+        scratch_shapes=[
+            pltpu.VMEM(kept.shape, kept.dtype),
+            pltpu.VMEM((rows, len(arrays) * cols), jnp.bfloat16),
+            pltpu.SemaphoreType.DMA((len(arrays),)),
+        ],
+        input_output_aliases={} if fresh else {1 + len(arrays): 0},
+        compiler_params=pltpu.CompilerParams(vmem_limit_bytes=PLACE_LIMIT),
+        cost_estimate=pl.CostEstimate(
+            flops=0, bytes_accessed=8 * rows * cols * len(arrays), transcendentals=0
+        ),
+        name="place",
+    )(table, *arrays, *(state or ()))
+
+
+def gate_kernel(x_ref, *refs):
+    pass
+
+
+def gate(x, *tokens):
+    return pl.pallas_call(
+        gate_kernel,
+        out_shape=jax.ShapeDtypeStruct(x.shape, x.dtype),
+        in_specs=[ANY] * (1 + len(tokens)),
+        out_specs=ANY,
+        input_output_aliases={0: 0},
+        compiler_params=pltpu.CompilerParams(vmem_limit_bytes=VMEM_LIMIT),
+        name="gate",
+    )(x, *tokens)
+
+
+def pairs(count, flip):
+    return [(i, i ^ flip) for i in range(count)]
+
+
+def paired(trainer_weight, dirty, rollout_owner, rollout_slot):
+    replicas, owners = lax.axis_size("rep"), lax.axis_size("exp")
+    local_count = trainer_weight.shape[0]
+
+    def over_rep(x, flip):
+        return lax.ppermute(x, "rep", pairs(replicas, flip))
+
+    picked = (4, 1, 2, 3, 5, 0, 6, 7)
+    outgoing = dict(zip(picked, pick(rollout_owner, trainer_weight, picked)))
+    table = routing_table(rollout_owner, dirty, rollout_slot, local_count)
+    after = {5: 1, 6: 3, 7: 4}
+    got, packed, state = {}, [], None
+    done = []
+    for group in GROUPS:
+        arrays, spots = [], []
+        for j in group:
+            for flip in ORDER[: LIMIT[j]]:
+                if flip not in got:
+                    x = outgoing[flip]
+                    if flip in after:
+                        x = gate(x, got[after[flip]])
+                    got[flip] = lax.ppermute(x, "exp", pairs(owners, flip)) if flip else x
+            final = j == CAP - 1
+            mine = pack(table, [got[f] for f in ORDER[: LIMIT[j]]], j, [packed[-1], done[0]] if final else [])
+            packed.append(mine)
+            beside = over_rep(mine, 1)
+            across = over_rep(mine, 2)
+            diagonal = over_rep(gate(across, done[-1]) if final else across, 1)
+            arrays += [mine, beside, across, diagonal]
+            spots += [(j, flip) for flip in range(4)]
+        state = place(state, table, arrays, tuple(spots), replicas, group == GROUPS[-1])
+        done.append(state[1])
+    tiles, scales = state
+    return tiles, scales[:, None, :]
 
 
 def quantize(weights):
@@ -17,7 +257,7 @@
     return (scaled, scale)
 
 
-def on_device(trainer_weight, dirty, rollout_owner, rollout_slot):
+def gathered(trainer_weight, dirty, rollout_owner, rollout_slot):
     owners = lax.axis_size("exp")
     here = lax.axis_index("exp")
     local_count = trainer_weight.shape[0]
@@ -69,6 +309,14 @@
     return (update_tiles, update_scales)
 
 
+def on_device(trainer_weight, dirty, rollout_owner, rollout_slot):
+    local_count, rows, cols = trainer_weight.shape
+    replicas, owners = lax.axis_size("rep"), lax.axis_size("exp")
+    if (replicas, owners, local_count, rows) == (4, len(ORDER), len(ORDER), B) and cols % B == 0:
+        return paired(trainer_weight, dirty, rollout_owner, rollout_slot)
+    return gathered(trainer_weight, dirty, rollout_owner, rollout_slot)
+
+
 def solution(mesh):
     in_specs = (P("exp", None, "rep"), P(), P(), P())
     out_specs = (P("exp", None, None), P("exp", None, None))

time: 227 us -> 118 us (0.52)
  waiting for transfers between devices: 159 us -> 64.4 us
  Pallas kernels: 0 us -> 20.3 us
  starting transfers between devices: 7.45 us -> 27.6 us
  blocking collectives: 15.1 us -> 0 us
  between operations: 14.1 us -> 0.8 us
  local copies, waits for them, and re-layouts: 15.6 us -> 4.03 us
  matrix products: 9.11 us -> 0 us
  other arithmetic: 6.35 us -> 0 us
    all_to_all x1 -> x0, waiting for transfers between devices: 81.6 us -> none  [on_device(): lax.all_to_all(send_tiles, 'exp', split_axis=0, concat_axis=0, tiled=True)]
    all_gather x1 -> x0, waiting for transfers between devices: 77.3 us -> none  [on_device(): lax.all_gather(tiles, 'rep', axis=2, tiled=True)]
    ppermute x0 -> x25, waiting for transfers between devices: none -> 64.4 us  [the longest x7 32.8 us: paired(): got[flip] = lax.ppermute(x, 'exp', pairs(owners, flip)) if flip else x]
    ppermute x0 -> x25, starting transfers between devices: none -> 27.6 us  [the longest x7 17.7 us: paired(): got[flip] = lax.ppermute(x, 'exp', pairs(owners, flip)) if flip else x]
    pallas_call x0 -> x15, Pallas kernels: none -> 20.3 us  [the longest x3 10.5 us: place(): pl.pallas_call(functools.partial(place_kernel, spots, fresh), out_shape=[...]
    all_to_all x1 -> x0, blocking collectives: 9.89 us -> none  [on_device(): lax.all_to_all(send_scales, 'exp', split_axis=0, concat_axis=0, tiled=True)]
    dot_general x5 -> x0, matrix products: 9.11 us -> none  [the longest x1 6.27 us: on_device(): jnp.einsum('cp,psd->csd', pick_low, got_tiles, preferred_element_type=jnp...]
    unnamed x6 -> x9, local copies, waits for them, and re-layouts: 12 us -> 4.03 us
  transfers between devices with their start and end apart: 2 -> 25, of which waited for: 2 -> 10; matrix products, arithmetic and copies ran while one was open for 1% -> 0% of each run, Pallas kernels for 0% -> 12%
where the time goes in v1:
time: 118 us; the launch traced here: 117 us
  waiting for transfers between devices  64.4 us (55%)
  starting transfers between devices  27.6 us (23%)
  Pallas kernels  20.3 us (17%)
  local copies, waits for them, and re-layouts  4.03 us (3%)
    ppermute x7, waiting for transfers between devices, paired(): got[flip] = lax.ppermute(x, 'exp', pairs(owners, flip)) if flip else x  32.8 us
    ppermute x18, waiting for transfers between devices, over_rep(): return lax.ppermute(x, 'rep', pairs(replicas, flip))  31.6 us
    ppermute x7, starting transfers between devices, paired(): got[flip] = lax.ppermute(x, 'exp', pairs(owners, flip)) if flip else x  17.7 us
    pallas_call x3, Pallas kernels, place(): pl.pallas_call(functools.partial(place_kernel, spots, fresh), out_shape=[...  10.5 us
    ppermute x18, starting transfers between devices, over_rep(): return lax.ppermute(x, 'rep', pairs(replicas, flip))  9.91 us
    pallas_call x6, Pallas kernels, pack(): pl.pallas_call(functools.partial(pack_kernel, j, len(arrived)), out_shape...  5.19 us
    unnamed x9, local copies, waits for them, and re-layouts  4.03 us
    pallas_call x1, Pallas kernels, pick(): pl.pallas_call(functools.partial(pick_kernel, shifts, local_count), out_s...  3.25 us
  transfers between devices with their start and end apart: 25, of which 10 were waited for; matrix products, arithmetic and copies ran while one was open for 0% of the time, Pallas kernels for 12%

profile of v1, /device:TPU:0, one launch (start us, length us, event | category | flops | bytes accessed | tf_op | source)
XLA Modules:
  0.0 117.1 jit_solution(8439874223917042334)
XLA Ops:
  0.6 2.0 %copy-done = bf16[8,128,1792]{2,1,0:T(8,128)(2,1)S(1)} copy-done((bf16[8,128,1792]{2,1,0:T(8,128)(2,1)S(1)}, bf16[8,128,1792]{2,1,0:T(8,128)(2,1)}, u32[]{:S(2)}) %copy-start) | copy-done | bytes 3670040
  2.7 0.7 copy-done.1
  3.3 3.2 %pick.1 = (bf16[128,1792]{1,0:T(8,128)(2,1)S(1)}, bf16[128,1792]{1,0:T(8,128)(2,1)S(1)}, bf16[128,1792]{1,0:T(8,128)(2,1)S(1)}, bf16[128,1792]{1,0:T(8,128)(2,1)...) custom-call(s32[64]{0:T(128)S(1)} %copy-done.1, ...), custom_call_target="tpu_custom_call" | custom-call | tf_op jit(solution)/shard_map/pick/pallas_call | solution.py:48
  6.6 3.0 %collective-permute-start = (bf16[128,1792]{1,0:T(8,128)(2,1)S(1)}, bf16[128,1792]{1,0:T(8,128)(2,1)S(1)}, u32[]{:S(2)}, u32[]{:S(2)}) collective-permute-start(bf16[128,1792]{1,0:T(8,128)(2,1)S(1)} %get-tuple-element.17), channel_id=1, source_target_pairs={{0,1},{1,0},{2,3},{3,2},{4,5},{5,4},{6,7},{7,6},{8,9},{9,8},{10,11... | collective-permute-start | bytes 1376264 | tf_op jit(solution)/shard_map/ppermute | solution.py:235
  9.6 1.6 %collective-permute-start.1 = (bf16[128,1792]{1,0:T(8,128)(2,1)S(1)}, bf16[128,1792]{1,0:T(8,128)(2,1)S(1)}, u32[]{:S(2)}, u32[]{:S(2)}) collective-permute-start(bf16[128,1792]{1,0:T(8,128)(2,1)S(1)} %get-tuple-element.18), channel_id=1, source_target_pairs={{0,2},{1,3},{2,0},{3,1},{4,6},{5,7},{6,4},{7,5},{8,10},{9,11},{10,... | collective-permute-start | bytes 1376264 | tf_op jit(solution)/shard_map/ppermute | solution.py:235
  11.2 0.0 collective-permute-start.2
  11.2 3.0 %collective-permute-start.3 = (bf16[128,1792]{1,0:T(8,128)(2,1)S(1)}, bf16[128,1792]{1,0:T(8,128)(2,1)S(1)}, u32[]{:S(2)}, u32[]{:S(2)}) collective-permute-start(bf16[128,1792]{1,0:T(8,128)(2,1)S(1)} %get-tuple-element.20), channel_id=1, source_target_pairs={{0,4},{1,5},{2,6},{3,7},{4,0},{5,1},{6,2},{7,3},{8,12},{9,13},{10,... | collective-permute-start | bytes 1376264 | tf_op jit(solution)/shard_map/ppermute | solution.py:235
  14.2 0.7 copy-done.2
  14.8 0.7 copy-done.3
  15.5 1.4 %routing_table.1.table_ref = s32[24]{0:T(128)S(1)} custom-call(s32[64]{0:T(128)S(1)} %copy-done.1, s32[64]{0:T(128)S(1)} %copy-done.2, s32[64]{0:T(128)S(1)} %copy-done.3), custom_call_target="tpu_custom_call" | custom-call | tf_op jit(solution)/shard_map/routing_table/pallas_call | solution.py:86
  16.8 3.3 %collective-permute-done.refs_0_.refs_1_ = bf16[128,1792]{1,0:T(8,128)(2,1)S(1)} collective-permute-done((bf16[128,1792]{1,0:T(8,128)(2,1)S(1)}, bf16[128,1792]{1,0:T(8,128)(2,1)S(1)}, u32[]{:S(2)}, u32[]{:S(2)}) %collective-permute-start) | collective-permute-done | bytes 458784 | tf_op jit(solution)/shard_map/ppermute | solution.py:235
  20.1 4.0 %collective-permute-start.4 = (bf16[128,1792]{1,0:T(8,128)(2,1)S(1)}, bf16[128,1792]{1,0:T(8,128)(2,1)S(1)}, u32[]{:S(2)}, u32[]{:S(2)}) collective-permute-start(bf16[128,1792]{1,0:T(8,128)(2,1)S(1)} %gate.4), channel_id=1, source_target_pairs={{0,5},{1,4},{2,7},{3,6},{4,1},{5,0},{6,3},{7,2},{8,13},{9,12},{10,... | collective-permute-start | bytes 1376264 | tf_op jit(solution)/shard_map/ppermute | solution.py:235
  24.2 18.4 %collective-permute-done.1.refs_2_ = bf16[128,1792]{1,0:T(8,128)(2,1)S(1)} collective-permute-done((bf16[128,1792]{1,0:T(8,128)(2,1)S(1)}, bf16[128,1792]{1,0:T(8,128)(2,1)S(1)}, u32[]{:S(2)}, u32[]{:S(2)}) %collective-permute-start.1) | collective-permute-done | bytes 458784 | tf_op jit(solution)/shard_map/ppermute | solution.py:235
  42.5 0.8 pack.7.refs_0_
  43.4 1.5 %collective-permute-start.8 = (bf16[128,1792]{1,0:T(8,128)(2,1)S(1)}, bf16[128,1792]{1,0:T(8,128)(2,1)S(1)}, u32[]{:S(2)}, u32[]{:S(2)}) collective-permute-start(bf16[128,1792]{1,0:T(8,128)(2,1)S(1)} %pack.7.refs_0_), channel_id=1, source_target_pairs={{0,16},{8,24},{16,0},{24,8},{1,17},{9,25},{17,1},{25,9},{2,18},{10... | collective-permute-start | bytes 1376264 | tf_op jit(solution)/shard_map/ppermute | solution.py:219
  44.9 0.0 collective-permute-start.7
  44.9 4.7 %collective-permute-done.2.refs_0_.refs_3_ = bf16[128,1792]{1,0:T(8,128)(2,1)S(1)} collective-permute-done((bf16[128,1792]{1,0:T(8,128)(2,1)S(1)}, bf16[128,1792]{1,0:T(8,128)(2,1)S(1)}, u32[]{:S(2)}, u32[]{:S(2)}) %collective-permute-start.2) | collective-permute-done | bytes 458784 | tf_op jit(solution)/shard_map/ppermute | solution.py:235
  49.6 0.9 pack.8.refs_4_
  50.5 1.7 %collective-permute-start.11 = (bf16[128,1792]{1,0:T(8,128)(2,1)S(1)}, bf16[128,1792]{1,0:T(8,128)(2,1)S(1)}, u32[]{:S(2)}, u32[]{:S(2)}) collective-permute-start(bf16[128,1792]{1,0:T(8,128)(2,1)S(1)} %pack.8.refs_4_), channel_id=1, source_target_pairs={{0,16},{8,24},{16,0},{24,8},{1,17},{9,25},{17,1},{25,9},{2,18},{10... | collective-permute-start | bytes 1376264 | tf_op jit(solution)/shard_map/ppermute | solution.py:219
  52.2 0.0 collective-permute-done.3.refs_0_.refs_4_
  52.2 0.0 collective-permute-start.10
  52.2 0.9 pack.9.refs_8_
  53.1 1.3 %collective-permute-done.4.refs_5_ = bf16[128,1792]{1,0:T(8,128)(2,1)S(1)} collective-permute-done((bf16[128,1792]{1,0:T(8,128)(2,1)S(1)}, bf16[128,1792]{1,0:T(8,128)(2,1)S(1)}, u32[]{:S(2)}, u32[]{:S(2)}) %collective-permute-start.4) | collective-permute-done | bytes 458784 | tf_op jit(solution)/shard_map/ppermute | solution.py:235
  54.4 1.5 %collective-permute-start.14 = (bf16[128,1792]{1,0:T(8,128)(2,1)S(1)}, bf16[128,1792]{1,0:T(8,128)(2,1)S(1)}, u32[]{:S(2)}, u32[]{:S(2)}) collective-permute-start(bf16[128,1792]{1,0:T(8,128)(2,1)S(1)} %pack.9.refs_8_), channel_id=1, source_target_pairs={{0,16},{8,24},{16,0},{24,8},{1,17},{9,25},{17,1},{25,9},{2,18},{10... | collective-permute-start | bytes 1376264 | tf_op jit(solution)/shard_map/ppermute | solution.py:219
  55.9 3.9 %collective-permute-start.5 = (bf16[128,1792]{1,0:T(8,128)(2,1)S(1)}, bf16[128,1792]{1,0:T(8,128)(2,1)S(1)}, u32[]{:S(2)}, u32[]{:S(2)}) collective-permute-start(bf16[128,1792]{1,0:T(8,128)(2,1)S(1)} %gate.5), channel_id=1, source_target_pairs={{0,6},{1,7},{2,4},{3,5},{4,2},{5,3},{6,0},{7,1},{8,14},{9,15},{10,... | collective-permute-start | bytes 1376264 | tf_op jit(solution)/shard_map/ppermute | solution.py:235
  59.8 4.2 %collective-permute-done.11.refs_6_ = bf16[128,1792]{1,0:T(8,128)(2,1)S(1)} collective-permute-done((bf16[128,1792]{1,0:T(8,128)(2,1)S(1)}, bf16[128,1792]{1,0:T(8,128)(2,1)S(1)}, u32[]{:S(2)}, u32[]{:S(2)}) %collective-permute-start.11) | collective-permute-done | bytes 458784 | tf_op jit(solution)/shard_map/ppermute | solution.py:219
  64.0 0.0 collective-permute-start.9
  64.0 0.5 collective-permute-start.12
  64.5 8.2 %collective-permute-done.14.refs_10_ = bf16[128,1792]{1,0:T(8,128)(2,1)S(1)} collective-permute-done((bf16[128,1792]{1,0:T(8,128)(2,1)S(1)}, bf16[128,1792]{1,0:T(8,128)(2,1)S(1)}, u32[]{:S(2)}, u32[]{:S(2)}) %collective-permute-start.14) | collective-permute-done | bytes 458784 | tf_op jit(solution)/shard_map/ppermute | solution.py:219
  72.7 0.0 collective-permute-start.15
  72.7 0.0 collective-permute-done.5.refs_6_
  72.7 2.2 %collective-permute-start.6 = (bf16[128,1792]{1,0:T(8,128)(2,1)S(1)}, bf16[128,1792]{1,0:T(8,128)(2,1)S(1)}, u32[]{:S(2)}, u32[]{:S(2)}) collective-permute-start(bf16[128,1792]{1,0:T(8,128)(2,1)S(1)} %gate.6), channel_id=1, source_target_pairs={{0,7},{1,6},{2,5},{3,4},{4,3},{5,2},{6,1},{7,0},{8,15},{9,14},{10,... | collective-permute-start | bytes 1376264 | tf_op jit(solution)/shard_map/ppermute | solution.py:235
  74.9 0.9 pack.11.refs_0_
  75.8 0.9 pack.6.refs_8_.refs_4_
  76.7 1.6 %collective-permute-start.19 = (bf16[128,1792]{1,0:T(8,128)(2,1)S(1)}, bf16[128,1792]{1,0:T(8,128)(2,1)S(1)}, u32[]{:S(2)}, u32[]{:S(2)}) collective-permute-start(bf16[128,1792]{1,0:T(8,128)(2,1)S(1)} %pack.11.refs_0_), channel_id=1, source_target_pairs={{0,16},{8,24},{16,0},{24,8},{1,17},{9,25},{17,1},{25,9},{2,18},{10... | collective-permute-start | bytes 1376264 | tf_op jit(solution)/shard_map/ppermute | solution.py:219
  78.3 0.5 collective-permute-start.22
  78.8 4.6 %place.3 = (bf16[6,128,7168]{2,1,0:T(8,128)(2,1)}, f32[8,128]{1,0:T(8,128)S(1)}) custom-call(s32[24]{0:T(128)S(1)} %routing_table.1.table_ref, bf16[128,1792]{1,0:T(8,128)(2,1)S(1)} %pack.7.refs_0_, bf16[128,1792]{1,0:T(8,128)(2,1)S(1)} %collective-permute-done.7.refs_1_, bf16[128,1792]{1,0:T(8,128)(2,1)S(1)} %collective-permute-done.8.refs_2_, ...), custom_call_target="tpu_custom_call" | custom-call | bytes 22020096 | tf_op jit(solution)/shard_map/place/pallas_call | solution.py:172
  83.4 5.1 %collective-permute-done.6.refs_7_ = bf16[128,1792]{1,0:T(8,128)(2,1)S(1)} collective-permute-done((bf16[128,1792]{1,0:T(8,128)(2,1)S(1)}, bf16[128,1792]{1,0:T(8,128)(2,1)S(1)}, u32[]{:S(2)}, u32[]{:S(2)}) %collective-permute-start.6) | collective-permute-done | bytes 458784 | tf_op jit(solution)/shard_map/ppermute | solution.py:235
  88.5 0.9 pack.10.refs_0_
  89.4 1.5 %collective-permute-start.17 = (bf16[128,1792]{1,0:T(8,128)(2,1)S(1)}, bf16[128,1792]{1,0:T(8,128)(2,1)S(1)}, u32[]{:S(2)}, u32[]{:S(2)}) collective-permute-start(bf16[128,1792]{1,0:T(8,128)(2,1)S(1)} %pack.10.refs_0_), channel_id=1, source_target_pairs={{0,16},{8,24},{16,0},{24,8},{1,17},{9,25},{17,1},{25,9},{2,18},{10... | collective-permute-start | bytes 1376264 | tf_op jit(solution)/shard_map/ppermute | solution.py:219
  90.9 0.5 collective-permute-start.21
  91.4 0.0 collective-permute-start.20
  91.4 8.6 %collective-permute-done.22.refs_6_ = bf16[128,1792]{1,0:T(8,128)(2,1)S(1)} collective-permute-done((bf16[128,1792]{1,0:T(8,128)(2,1)S(1)}, bf16[128,1792]{1,0:T(8,128)(2,1)S(1)}, u32[]{:S(2)}, u32[]{:S(2)}) %collective-permute-start.22) | collective-permute-done | bytes 458784 | tf_op jit(solution)/shard_map/ppermute | solution.py:219
  100.0 9.1 %collective-permute-done.17.refs_2_ = bf16[128,1792]{1,0:T(8,128)(2,1)S(1)} collective-permute-done((bf16[128,1792]{1,0:T(8,128)(2,1)S(1)}, bf16[128,1792]{1,0:T(8,128)(2,1)S(1)}, u32[]{:S(2)}, u32[]{:S(2)}) %collective-permute-start.17) | collective-permute-done | bytes 458784 | tf_op jit(solution)/shard_map/ppermute | solution.py:219
  109.2 3.5 %place.4 = (bf16[6,128,7168]{2,1,0:T(8,128)(2,1)}, f32[8,128]{1,0:T(8,128)S(1)}) custom-call(s32[24]{0:T(128)S(1)} %routing_table.1.table_ref, bf16[128,1792]{1,0:T(8,128)(2,1)S(1)} %pack.11.refs_0_, bf16[128,1792]{1,0:T(8,128)(2,1)S(1)} %collective-permute-done.18.refs_1_, ...), custom_call_target="tpu_custom_call", output_to_operand_aliasing={{0}: (9, {})} | custom-call | bytes 14680064 | tf_op jit(solution)/shard_map/place/pallas_call | solution.py:172
  112.7 0.6 collective-permute-start.24
  113.3 1.4 %collective-permute-done.24.refs_3_ = bf16[128,1792]{1,0:T(8,128)(2,1)S(1)} collective-permute-done((bf16[128,1792]{1,0:T(8,128)(2,1)S(1)}, bf16[128,1792]{1,0:T(8,128)(2,1)S(1)}, u32[]{:S(2)}, u32[]{:S(2)}) %collective-permute-start.24) | collective-permute-done | bytes 458784 | tf_op jit(solution)/shard_map/ppermute | solution.py:219
  114.7 2.4 %place.5 = (bf16[6,128,7168]{2,1,0:T(8,128)(2,1)}, bf16[6,56]{1,0:T(8,128)(2,1)}) custom-call(s32[24]{0:T(128)S(1)} %routing_table.1.table_ref, bf16[128,1792]{1,0:T(8,128)(2,1)S(1)} %pack.10.refs_0_, bf16[128,1792]{1,0:T(8,128)(2,1)S(1)} %collective-permute-done.16.refs_1_, ...), custom_call_target="tpu_custom_call", output_to_operand_aliasing={{0}: (5, {})} | custom-call | bytes 7340032 | tf_op jit(solution)/shard_map/place/pallas_call | solution.py:172
  (26 shorter events, 0.1 us)
Async XLA Ops:
  0.6 2.0 %copy-start = (bf16[8,128,1792]{2,1,0:T(8,128)(2,1)S(1)}, bf16[8,128,1792]{2,1,0:T(8,128)(2,1)}, u32[]{:S(2)}) copy-start(bf16[8,128,1792]{2,1,0:T(8,128)(2,1)} %w_ref.1) | copy-start | bytes 11010052
  2.7 0.7 copy-start.1
  6.6 13.6 %collective-permute-start = (bf16[128,1792]{1,0:T(8,128)(2,1)S(1)}, bf16[128,1792]{1,0:T(8,128)(2,1)S(1)}, u32[]{:S(2)}, u32[]{:S(2)}) collective-permute-start(bf16[128,1792]{1,0:T(8,128)(2,1)S(1)} %get-tuple-element.17), channel_id=1, source_target_pairs={{0,1},{1,0},{2,3},{3,2},{4,5},{5,4},{6,7},{7,6},{8,9},{9,8},{10,11... | collective-permute-start | bytes 1376264 | tf_op jit(solution)/shard_map/ppermute | solution.py:235
  9.6 32.9 %collective-permute-start.1 = (bf16[128,1792]{1,0:T(8,128)(2,1)S(1)}, bf16[128,1792]{1,0:T(8,128)(2,1)S(1)}, u32[]{:S(2)}, u32[]{:S(2)}) collective-permute-start(bf16[128,1792]{1,0:T(8,128)(2,1)S(1)} %get-tuple-element.18), channel_id=1, source_target_pairs={{0,2},{1,3},{2,0},{3,1},{4,6},{5,7},{6,4},{7,5},{8,10},{9,11},{10,... | collective-permute-start | bytes 1376264 | tf_op jit(solution)/shard_map/ppermute | solution.py:235
  11.2 38.5 %collective-permute-start.2 = (bf16[128,1792]{1,0:T(8,128)(2,1)S(1)}, bf16[128,1792]{1,0:T(8,128)(2,1)S(1)}, u32[]{:S(2)}, u32[]{:S(2)}) collective-permute-start(bf16[128,1792]{1,0:T(8,128)(2,1)S(1)} %get-tuple-element.19), channel_id=1, source_target_pairs={{0,3},{1,2},{2,1},{3,0},{4,7},{5,6},{6,5},{7,4},{8,11},{9,10},{10,... | collective-permute-start | bytes 1376264 | tf_op jit(solution)/shard_map/ppermute | solution.py:235
  11.2 41.0 %collective-permute-start.3 = (bf16[128,1792]{1,0:T(8,128)(2,1)S(1)}, bf16[128,1792]{1,0:T(8,128)(2,1)S(1)}, u32[]{:S(2)}, u32[]{:S(2)}) collective-permute-start(bf16[128,1792]{1,0:T(8,128)(2,1)S(1)} %get-tuple-element.20), channel_id=1, source_target_pairs={{0,4},{1,5},{2,6},{3,7},{4,0},{5,1},{6,2},{7,3},{8,12},{9,13},{10,... | collective-permute-start | bytes 1376264 | tf_op jit(solution)/shard_map/ppermute | solution.py:235
  14.2 0.7 copy-start.2
  14.8 0.7 copy-start.3
  20.1 34.3 %collective-permute-start.4 = (bf16[128,1792]{1,0:T(8,128)(2,1)S(1)}, bf16[128,1792]{1,0:T(8,128)(2,1)S(1)}, u32[]{:S(2)}, u32[]{:S(2)}) collective-permute-start(bf16[128,1792]{1,0:T(8,128)(2,1)S(1)} %gate.4), channel_id=1, source_target_pairs={{0,5},{1,4},{2,7},{3,6},{4,1},{5,0},{6,3},{7,2},{8,13},{9,12},{10,... | collective-permute-start | bytes 1376264 | tf_op jit(solution)/shard_map/ppermute | solution.py:235
  43.4 12.5 %collective-permute-start.8 = (bf16[128,1792]{1,0:T(8,128)(2,1)S(1)}, bf16[128,1792]{1,0:T(8,128)(2,1)S(1)}, u32[]{:S(2)}, u32[]{:S(2)}) collective-permute-start(bf16[128,1792]{1,0:T(8,128)(2,1)S(1)} %pack.7.refs_0_), channel_id=1, source_target_pairs={{0,16},{8,24},{16,0},{24,8},{1,17},{9,25},{17,1},{25,9},{2,18},{10... | collective-permute-start | bytes 1376264 | tf_op jit(solution)/shard_map/ppermute | solution.py:219
  44.9 14.9 %collective-permute-start.7 = (bf16[128,1792]{1,0:T(8,128)(2,1)S(1)}, bf16[128,1792]{1,0:T(8,128)(2,1)S(1)}, u32[]{:S(2)}, u32[]{:S(2)}) collective-permute-start(bf16[128,1792]{1,0:T(8,128)(2,1)S(1)} %pack.7.refs_0_), channel_id=1, source_target_pairs={{0,8},{8,0},{16,24},{24,16},{1,9},{9,1},{17,25},{25,17},{2,10},{10... | collective-permute-start | bytes 1376264 | tf_op jit(solution)/shard_map/ppermute | solution.py:219
  50.5 13.5 %collective-permute-start.11 = (bf16[128,1792]{1,0:T(8,128)(2,1)S(1)}, bf16[128,1792]{1,0:T(8,128)(2,1)S(1)}, u32[]{:S(2)}, u32[]{:S(2)}) collective-permute-start(bf16[128,1792]{1,0:T(8,128)(2,1)S(1)} %pack.8.refs_4_), channel_id=1, source_target_pairs={{0,16},{8,24},{16,0},{24,8},{1,17},{9,25},{17,1},{25,9},{2,18},{10... | collective-permute-start | bytes 1376264 | tf_op jit(solution)/shard_map/ppermute | solution.py:219
  52.2 11.8 %collective-permute-start.10 = (bf16[128,1792]{1,0:T(8,128)(2,1)S(1)}, bf16[128,1792]{1,0:T(8,128)(2,1)S(1)}, u32[]{:S(2)}, u32[]{:S(2)}) collective-permute-start(bf16[128,1792]{1,0:T(8,128)(2,1)S(1)} %pack.8.refs_4_), channel_id=1, source_target_pairs={{0,8},{8,0},{16,24},{24,16},{1,9},{9,1},{17,25},{25,17},{2,10},{10... | collective-permute-start | bytes 1376264 | tf_op jit(solution)/shard_map/ppermute | solution.py:219
  54.4 18.3 %collective-permute-start.14 = (bf16[128,1792]{1,0:T(8,128)(2,1)S(1)}, bf16[128,1792]{1,0:T(8,128)(2,1)S(1)}, u32[]{:S(2)}, u32[]{:S(2)}) collective-permute-start(bf16[128,1792]{1,0:T(8,128)(2,1)S(1)} %pack.9.refs_8_), channel_id=1, source_target_pairs={{0,16},{8,24},{16,0},{24,8},{1,17},{9,25},{17,1},{25,9},{2,18},{10... | collective-permute-start | bytes 1376264 | tf_op jit(solution)/shard_map/ppermute | solution.py:219
  55.9 16.8 %collective-permute-start.5 = (bf16[128,1792]{1,0:T(8,128)(2,1)S(1)}, bf16[128,1792]{1,0:T(8,128)(2,1)S(1)}, u32[]{:S(2)}, u32[]{:S(2)}) collective-permute-start(bf16[128,1792]{1,0:T(8,128)(2,1)S(1)} %gate.5), channel_id=1, source_target_pairs={{0,6},{1,7},{2,4},{3,5},{4,2},{5,3},{6,0},{7,1},{8,14},{9,15},{10,... | collective-permute-start | bytes 1376264 | tf_op jit(solution)/shard_map/ppermute | solution.py:235
  59.8 16.9 %collective-permute-start.13 = (bf16[128,1792]{1,0:T(8,128)(2,1)S(1)}, bf16[128,1792]{1,0:T(8,128)(2,1)S(1)}, u32[]{:S(2)}, u32[]{:S(2)}) collective-permute-start(bf16[128,1792]{1,0:T(8,128)(2,1)S(1)} %pack.9.refs_8_), channel_id=1, source_target_pairs={{0,8},{8,0},{16,24},{24,16},{1,9},{9,1},{17,25},{25,17},{2,10},{10... | collective-permute-start | bytes 1376264 | tf_op jit(solution)/shard_map/ppermute | solution.py:219
  64.0 14.3 %collective-permute-start.9 = (bf16[128,1792]{1,0:T(8,128)(2,1)S(1)}, bf16[128,1792]{1,0:T(8,128)(2,1)S(1)}, u32[]{:S(2)}, u32[]{:S(2)}) collective-permute-start(bf16[128,1792]{1,0:T(8,128)(2,1)S(1)} %collective-permute-done.8.refs_2_), channel_id=1, source_target_pairs={{0,8},{8,0},{16,24},{24,16},{1,9},{9,1},{17,25},{25,17},{2,10},{10... | collective-permute-start | bytes 1376264 | tf_op jit(solution)/shard_map/ppermute | solution.py:219
  64.0 14.8 %collective-permute-start.12 = (bf16[128,1792]{1,0:T(8,128)(2,1)S(1)}, bf16[128,1792]{1,0:T(8,128)(2,1)S(1)}, u32[]{:S(2)}, u32[]{:S(2)}) collective-permute-start(bf16[128,1792]{1,0:T(8,128)(2,1)S(1)} %collective-permute-done.11.refs_6_), channel_id=1, source_target_pairs={{0,8},{8,0},{16,24},{24,16},{1,9},{9,1},{17,25},{25,17},{2,10},{10... | collective-permute-start | bytes 1376264 | tf_op jit(solution)/shard_map/ppermute | solution.py:219
  72.7 6.1 %collective-permute-start.15 = (bf16[128,1792]{1,0:T(8,128)(2,1)S(1)}, bf16[128,1792]{1,0:T(8,128)(2,1)S(1)}, u32[]{:S(2)}, u32[]{:S(2)}) collective-permute-start(bf16[128,1792]{1,0:T(8,128)(2,1)S(1)} %collective-permute-done.14.refs_10_), channel_id=1, source_target_pairs={{0,8},{8,0},{16,24},{24,16},{1,9},{9,1},{17,25},{25,17},{2,10},{10... | collective-permute-start | bytes 1376264 | tf_op jit(solution)/shard_map/ppermute | solution.py:219
  72.7 15.7 %collective-permute-start.6 = (bf16[128,1792]{1,0:T(8,128)(2,1)S(1)}, bf16[128,1792]{1,0:T(8,128)(2,1)S(1)}, u32[]{:S(2)}, u32[]{:S(2)}) collective-permute-start(bf16[128,1792]{1,0:T(8,128)(2,1)S(1)} %gate.6), channel_id=1, source_target_pairs={{0,7},{1,6},{2,5},{3,4},{4,3},{5,2},{6,1},{7,0},{8,15},{9,14},{10,... | collective-permute-start | bytes 1376264 | tf_op jit(solution)/shard_map/ppermute | solution.py:235
  76.7 14.7 %collective-permute-start.19 = (bf16[128,1792]{1,0:T(8,128)(2,1)S(1)}, bf16[128,1792]{1,0:T(8,128)(2,1)S(1)}, u32[]{:S(2)}, u32[]{:S(2)}) collective-permute-start(bf16[128,1792]{1,0:T(8,128)(2,1)S(1)} %pack.11.refs_0_), channel_id=1, source_target_pairs={{0,16},{8,24},{16,0},{24,8},{1,17},{9,25},{17,1},{25,9},{2,18},{10... | collective-permute-start | bytes 1376264 | tf_op jit(solution)/shard_map/ppermute | solution.py:219
  78.3 21.7 %collective-permute-start.22 = (bf16[128,1792]{1,0:T(8,128)(2,1)S(1)}, bf16[128,1792]{1,0:T(8,128)(2,1)S(1)}, u32[]{:S(2)}, u32[]{:S(2)}) collective-permute-start(bf16[128,1792]{1,0:T(8,128)(2,1)S(1)} %pack.6.refs_8_.refs_4_), channel_id=1, source_target_pairs={{0,16},{8,24},{16,0},{24,8},{1,17},{9,25},{17,1},{25,9},{2,18},{10... | collective-permute-start | bytes 1376264 | tf_op jit(solution)/shard_map/ppermute | solution.py:219
  89.4 19.7 %collective-permute-start.17 = (bf16[128,1792]{1,0:T(8,128)(2,1)S(1)}, bf16[128,1792]{1,0:T(8,128)(2,1)S(1)}, u32[]{:S(2)}, u32[]{:S(2)}) collective-permute-start(bf16[128,1792]{1,0:T(8,128)(2,1)S(1)} %pack.10.refs_0_), channel_id=1, source_target_pairs={{0,16},{8,24},{16,0},{24,8},{1,17},{9,25},{17,1},{25,9},{2,18},{10... | collective-permute-start | bytes 1376264 | tf_op jit(solution)/shard_map/ppermute | solution.py:219
  90.9 18.3 %collective-permute-start.18 = (bf16[128,1792]{1,0:T(8,128)(2,1)S(1)}, bf16[128,1792]{1,0:T(8,128)(2,1)S(1)}, u32[]{:S(2)}, u32[]{:S(2)}) collective-permute-start(bf16[128,1792]{1,0:T(8,128)(2,1)S(1)} %pack.11.refs_0_), channel_id=1, source_target_pairs={{0,8},{8,0},{16,24},{24,16},{1,9},{9,1},{17,25},{25,17},{2,10},{10... | collective-permute-start | bytes 1376264 | tf_op jit(solution)/shard_map/ppermute | solution.py:219
  90.9 18.3 %collective-permute-start.21 = (bf16[128,1792]{1,0:T(8,128)(2,1)S(1)}, bf16[128,1792]{1,0:T(8,128)(2,1)S(1)}, u32[]{:S(2)}, u32[]{:S(2)}) collective-permute-start(bf16[128,1792]{1,0:T(8,128)(2,1)S(1)} %pack.6.refs_8_.refs_4_), channel_id=1, source_target_pairs={{0,8},{8,0},{16,24},{24,16},{1,9},{9,1},{17,25},{25,17},{2,10},{10... | collective-permute-start | bytes 1376264 | tf_op jit(solution)/shard_map/ppermute | solution.py:219
  91.4 17.8 %collective-permute-start.20 = (bf16[128,1792]{1,0:T(8,128)(2,1)S(1)}, bf16[128,1792]{1,0:T(8,128)(2,1)S(1)}, u32[]{:S(2)}, u32[]{:S(2)}) collective-permute-start(bf16[128,1792]{1,0:T(8,128)(2,1)S(1)} %collective-permute-done.19.refs_2_), channel_id=1, source_target_pairs={{0,8},{8,0},{16,24},{24,16},{1,9},{9,1},{17,25},{25,17},{2,10},{10... | collective-permute-start | bytes 1376264 | tf_op jit(solution)/shard_map/ppermute | solution.py:219
  100.0 9.2 %collective-permute-start.23 = (bf16[128,1792]{1,0:T(8,128)(2,1)S(1)}, bf16[128,1792]{1,0:T(8,128)(2,1)S(1)}, u32[]{:S(2)}, u32[]{:S(2)}) collective-permute-start(bf16[128,1792]{1,0:T(8,128)(2,1)S(1)} %collective-permute-done.22.refs_6_), channel_id=1, source_target_pairs={{0,8},{8,0},{16,24},{24,16},{1,9},{9,1},{17,25},{25,17},{2,10},{10... | collective-permute-start | bytes 1376264 | tf_op jit(solution)/shard_map/ppermute | solution.py:219
  109.1 4.2 %collective-permute-start.16 = (bf16[128,1792]{1,0:T(8,128)(2,1)S(1)}, bf16[128,1792]{1,0:T(8,128)(2,1)S(1)}, u32[]{:S(2)}, u32[]{:S(2)}) collective-permute-start(bf16[128,1792]{1,0:T(8,128)(2,1)S(1)} %pack.10.refs_0_), channel_id=1, source_target_pairs={{0,8},{8,0},{16,24},{24,16},{1,9},{9,1},{17,25},{25,17},{2,10},{10... | collective-permute-start | bytes 1376264 | tf_op jit(solution)/shard_map/ppermute | solution.py:219
  112.7 2.0 %collective-permute-start.24 = (bf16[128,1792]{1,0:T(8,128)(2,1)S(1)}, bf16[128,1792]{1,0:T(8,128)(2,1)S(1)}, u32[]{:S(2)}, u32[]{:S(2)}) collective-permute-start(bf16[128,1792]{1,0:T(8,128)(2,1)S(1)} %gate.7), channel_id=1, source_target_pairs={{0,8},{8,0},{16,24},{24,16},{1,9},{9,1},{17,25},{25,17},{2,10},{10... | collective-permute-start | bytes 1376264 | tf_op jit(solution)/shard_map/ppermute | solution.py:219

commit v2 on v1

--- a/solution.py
+++ b/solution.py
@@ -10,9 +10,10 @@
 B = 128
 CAP = 6
 
-ORDER = (0, 1, 2, 3, 4, 5, 6, 7)
+ORDER = (0, 1, 2, 3, 4, 5, 7, 6)
 LIMIT = (3, 4, 5, 6, 7, 8)
-GROUPS = ((0, 1, 2), (3, 4), (5,))
+ALL = (0, 1, 2, 3)
+WAVES = (((0, ALL), (1, ALL), (2, ALL)), ((3, ALL), (4, ALL), (5, (0, 1))), ((5, (2, 3)),))
 PICK, ROW, LIVE = 0, 8, 16
 VMEM_LIMIT = 8 * 1024 * 1024
 PLACE_LIMIT = 24 * 1024 * 1024
@@ -218,31 +219,33 @@
     def over_rep(x, flip):
         return lax.ppermute(x, "rep", pairs(replicas, flip))
 
-    picked = (4, 1, 2, 3, 5, 0, 6, 7)
+    picked = (4, 1, 2, 3, 5, 0, 7, 6)
     outgoing = dict(zip(picked, pick(rollout_owner, trainer_weight, picked)))
     table = routing_table(rollout_owner, dirty, rollout_slot, local_count)
-    after = {5: 1, 6: 3, 7: 4}
-    got, packed, state = {}, [], None
-    done = []
-    for group in GROUPS:
-        arrays, spots = [], []
-        for j in group:
-            for flip in ORDER[: LIMIT[j]]:
-                if flip not in got:
-                    x = outgoing[flip]
-                    if flip in after:
-                        x = gate(x, got[after[flip]])
-                    got[flip] = lax.ppermute(x, "exp", pairs(owners, flip)) if flip else x
-            final = j == CAP - 1
-            mine = pack(table, [got[f] for f in ORDER[: LIMIT[j]]], j, [packed[-1], done[0]] if final else [])
-            packed.append(mine)
-            beside = over_rep(mine, 1)
-            across = over_rep(mine, 2)
-            diagonal = over_rep(gate(across, done[-1]) if final else across, 1)
-            arrays += [mine, beside, across, diagonal]
-            spots += [(j, flip) for flip in range(4)]
-        state = place(state, table, arrays, tuple(spots), replicas, group == GROUPS[-1])
-        done.append(state[1])
+    after = {5: 1, 7: 3, 6: 4}
+    got, held, state = {}, {}, None
+
+    def arrival(flip):
+        if flip not in got:
+            x = outgoing[flip]
+            if flip in after:
+                x = gate(x, got[after[flip]])
+            got[flip] = lax.ppermute(x, "exp", pairs(owners, flip)) if flip else x
+        return got[flip]
+
+    def shard(j, flip):
+        if (j, flip) not in held:
+            if flip == 0:
+                tokens = [held[j - 1, 0], state[1]] if j == CAP - 1 else []
+                held[j, 0] = pack(table, [arrival(f) for f in ORDER[: LIMIT[j]]], j, tokens)
+            else:
+                held[j, flip] = over_rep(held[j, 2 if flip == 3 else 0], 1 if flip & 1 else 2)
+        return held[j, flip]
+
+    for wave in WAVES:
+        spots = tuple((j, flip) for j, flips in wave for flip in flips)
+        arrays = [shard(j, flip) for j, flip in spots]
+        state = place(state, table, arrays, spots, replicas, wave is WAVES[-1])
     tiles, scales = state
     return tiles, scales[:, None, :]
 

time: 118 us -> 115 us (0.975)
  waiting for transfers between devices: 64.4 us -> 62.7 us
  starting transfers between devices: 27.6 us -> 26.4 us
    ppermute x18, waiting for transfers between devices: 31.6 us -> 30 us  [over_rep(): return lax.ppermute(x, 'rep', pairs(replicas, flip))]
    ppermute x7, starting transfers between devices: 17.7 us -> 16.5 us  [arrival(): got[flip] = lax.ppermute(x, 'exp', pairs(owners, flip)) if flip else x]
    unnamed x9 -> x8, local copies, waits for them, and re-layouts: 4.03 us -> 4 us
  transfers between devices with their start and end apart: 25 -> 25, of which waited for: 10 -> 9; matrix products, arithmetic and copies ran while one was open for 0% -> 0% of each run, Pallas kernels for 12% -> 13%
where the time goes in v2:
time: 115 us; the launch traced here: 114 us
  waiting for transfers between devices  62.7 us (55%)
  starting transfers between devices  26.4 us (23%)
  Pallas kernels  20.5 us (18%)
  local copies, waits for them, and re-layouts  4 us (3%)
    ppermute x7, waiting for transfers between devices, arrival(): got[flip] = lax.ppermute(x, 'exp', pairs(owners, flip)) if flip else x  32.7 us
    ppermute x18, waiting for transfers between devices, over_rep(): return lax.ppermute(x, 'rep', pairs(replicas, flip))  30 us
    ppermute x7, starting transfers between devices, arrival(): got[flip] = lax.ppermute(x, 'exp', pairs(owners, flip)) if flip else x  16.5 us
    pallas_call x3, Pallas kernels, place(): pl.pallas_call(functools.partial(place_kernel, spots, fresh), out_shape=[...  10.7 us
    ppermute x18, starting transfers between devices, over_rep(): return lax.ppermute(x, 'rep', pairs(replicas, flip))  9.91 us
    pallas_call x6, Pallas kernels, pack(): pl.pallas_call(functools.partial(pack_kernel, j, len(arrived)), out_shape...  5.19 us
    unnamed x8, local copies, waits for them, and re-layouts  4 us
    pallas_call x1, Pallas kernels, pick(): pl.pallas_call(functools.partial(pick_kernel, shifts, local_count), out_s...  3.25 us
  transfers between devices with their start and end apart: 25, of which 9 were waited for; matrix products, arithmetic and copies ran while one was open for 0% of the time, Pallas kernels for 13%

profile of v2, /device:TPU:0, one launch (start us, length us, event | category | flops | bytes accessed | tf_op | source)
XLA Modules:
  0.0 114.4 jit_solution(4106186184144156018)
XLA Ops:
  0.6 2.0 %copy-done = bf16[8,128,1792]{2,1,0:T(8,128)(2,1)S(1)} copy-done((bf16[8,128,1792]{2,1,0:T(8,128)(2,1)S(1)}, bf16[8,128,1792]{2,1,0:T(8,128)(2,1)}, u32[]{:S(2)}) %copy-start) | copy-done | bytes 3670040
  2.7 0.7 copy-done.1
  3.3 3.2 %pick.1 = (bf16[128,1792]{1,0:T(8,128)(2,1)S(1)}, bf16[128,1792]{1,0:T(8,128)(2,1)S(1)}, bf16[128,1792]{1,0:T(8,128)(2,1)S(1)}, bf16[128,1792]{1,0:T(8,128)(2,1)...) custom-call(s32[64]{0:T(128)S(1)} %copy-done.1, ...), custom_call_target="tpu_custom_call" | custom-call | tf_op jit(solution)/shard_map/pick/pallas_call | solution.py:49
  6.6 3.0 %collective-permute-start = (bf16[128,1792]{1,0:T(8,128)(2,1)S(1)}, bf16[128,1792]{1,0:T(8,128)(2,1)S(1)}, u32[]{:S(2)}, u32[]{:S(2)}) collective-permute-start(bf16[128,1792]{1,0:T(8,128)(2,1)S(1)} %get-tuple-element.17), channel_id=1, source_target_pairs={{0,1},{1,0},{2,3},{3,2},{4,5},{5,4},{6,7},{7,6},{8,9},{9,8},{10,11... | collective-permute-start | bytes 1376264 | tf_op jit(solution)/shard_map/ppermute | solution.py:233
  9.6 1.6 %collective-permute-start.1 = (bf16[128,1792]{1,0:T(8,128)(2,1)S(1)}, bf16[128,1792]{1,0:T(8,128)(2,1)S(1)}, u32[]{:S(2)}, u32[]{:S(2)}) collective-permute-start(bf16[128,1792]{1,0:T(8,128)(2,1)S(1)} %get-tuple-element.18), channel_id=1, source_target_pairs={{0,2},{1,3},{2,0},{3,1},{4,6},{5,7},{6,4},{7,5},{8,10},{9,11},{10,... | collective-permute-start | bytes 1376264 | tf_op jit(solution)/shard_map/ppermute | solution.py:233
  11.2 0.0 collective-permute-start.2
  11.2 3.0 %collective-permute-start.3 = (bf16[128,1792]{1,0:T(8,128)(2,1)S(1)}, bf16[128,1792]{1,0:T(8,128)(2,1)S(1)}, u32[]{:S(2)}, u32[]{:S(2)}) collective-permute-start(bf16[128,1792]{1,0:T(8,128)(2,1)S(1)} %get-tuple-element.20), channel_id=1, source_target_pairs={{0,4},{1,5},{2,6},{3,7},{4,0},{5,1},{6,2},{7,3},{8,12},{9,13},{10,... | collective-permute-start | bytes 1376264 | tf_op jit(solution)/shard_map/ppermute | solution.py:233
  14.2 0.7 copy-done.2
  14.8 0.7 copy-done.3
  15.5 1.4 %routing_table.1.table_ref = s32[24]{0:T(128)S(1)} custom-call(s32[64]{0:T(128)S(1)} %copy-done.1, s32[64]{0:T(128)S(1)} %copy-done.2, s32[64]{0:T(128)S(1)} %copy-done.3), custom_call_target="tpu_custom_call" | custom-call | tf_op jit(solution)/shard_map/routing_table/pallas_call | solution.py:87
  16.8 3.3 %collective-permute-done.refs_0_.refs_1_ = bf16[128,1792]{1,0:T(8,128)(2,1)S(1)} collective-permute-done((bf16[128,1792]{1,0:T(8,128)(2,1)S(1)}, bf16[128,1792]{1,0:T(8,128)(2,1)S(1)}, u32[]{:S(2)}, u32[]{:S(2)}) %collective-permute-start) | collective-permute-done | bytes 458784 | tf_op jit(solution)/shard_map/ppermute | solution.py:233
  20.1 4.0 %collective-permute-start.4 = (bf16[128,1792]{1,0:T(8,128)(2,1)S(1)}, bf16[128,1792]{1,0:T(8,128)(2,1)S(1)}, u32[]{:S(2)}, u32[]{:S(2)}) collective-permute-start(bf16[128,1792]{1,0:T(8,128)(2,1)S(1)} %gate.3), channel_id=1, source_target_pairs={{0,5},{1,4},{2,7},{3,6},{4,1},{5,0},{6,3},{7,2},{8,13},{9,12},{10,... | collective-permute-start | bytes 1376264 | tf_op jit(solution)/shard_map/ppermute | solution.py:233
  24.2 18.4 %collective-permute-done.1.refs_2_ = bf16[128,1792]{1,0:T(8,128)(2,1)S(1)} collective-permute-done((bf16[128,1792]{1,0:T(8,128)(2,1)S(1)}, bf16[128,1792]{1,0:T(8,128)(2,1)S(1)}, u32[]{:S(2)}, u32[]{:S(2)}) %collective-permute-start.1) | collective-permute-done | bytes 458784 | tf_op jit(solution)/shard_map/ppermute | solution.py:233
  42.5 0.8 pack.7.refs_0_
  43.4 1.5 %collective-permute-start.8 = (bf16[128,1792]{1,0:T(8,128)(2,1)S(1)}, bf16[128,1792]{1,0:T(8,128)(2,1)S(1)}, u32[]{:S(2)}, u32[]{:S(2)}) collective-permute-start(bf16[128,1792]{1,0:T(8,128)(2,1)S(1)} %pack.7.refs_0_), channel_id=1, source_target_pairs={{0,16},{8,24},{16,0},{24,8},{1,17},{9,25},{17,1},{25,9},{2,18},{10... | collective-permute-start | bytes 1376264 | tf_op jit(solution)/shard_map/ppermute | solution.py:220
  44.9 0.0 collective-permute-start.7
  44.9 4.7 %collective-permute-done.2.refs_0_.refs_3_ = bf16[128,1792]{1,0:T(8,128)(2,1)S(1)} collective-permute-done((bf16[128,1792]{1,0:T(8,128)(2,1)S(1)}, bf16[128,1792]{1,0:T(8,128)(2,1)S(1)}, u32[]{:S(2)}, u32[]{:S(2)}) %collective-permute-start.2) | collective-permute-done | bytes 458784 | tf_op jit(solution)/shard_map/ppermute | solution.py:233
  49.6 0.9 pack.8.refs_4_
  50.5 1.7 %collective-permute-start.11 = (bf16[128,1792]{1,0:T(8,128)(2,1)S(1)}, bf16[128,1792]{1,0:T(8,128)(2,1)S(1)}, u32[]{:S(2)}, u32[]{:S(2)}) collective-permute-start(bf16[128,1792]{1,0:T(8,128)(2,1)S(1)} %pack.8.refs_4_), channel_id=1, source_target_pairs={{0,16},{8,24},{16,0},{24,8},{1,17},{9,25},{17,1},{25,9},{2,18},{10... | collective-permute-start | bytes 1376264 | tf_op jit(solution)/shard_map/ppermute | solution.py:220
  52.2 0.0 collective-permute-done.3.refs_0_.refs_4_
  52.2 0.0 collective-permute-start.10
  52.2 0.9 pack.9.refs_8_
  53.1 1.3 %collective-permute-done.4.refs_5_ = bf16[128,1792]{1,0:T(8,128)(2,1)S(1)} collective-permute-done((bf16[128,1792]{1,0:T(8,128)(2,1)S(1)}, bf16[128,1792]{1,0:T(8,128)(2,1)S(1)}, u32[]{:S(2)}, u32[]{:S(2)}) %collective-permute-start.4) | collective-permute-done | bytes 458784 | tf_op jit(solution)/shard_map/ppermute | solution.py:233
  54.4 1.5 %collective-permute-start.14 = (bf16[128,1792]{1,0:T(8,128)(2,1)S(1)}, bf16[128,1792]{1,0:T(8,128)(2,1)S(1)}, u32[]{:S(2)}, u32[]{:S(2)}) collective-permute-start(bf16[128,1792]{1,0:T(8,128)(2,1)S(1)} %pack.9.refs_8_), channel_id=1, source_target_pairs={{0,16},{8,24},{16,0},{24,8},{1,17},{9,25},{17,1},{25,9},{2,18},{10... | collective-permute-start | bytes 1376264 | tf_op jit(solution)/shard_map/ppermute | solution.py:220
  55.9 3.5 %collective-permute-start.5 = (bf16[128,1792]{1,0:T(8,128)(2,1)S(1)}, bf16[128,1792]{1,0:T(8,128)(2,1)S(1)}, u32[]{:S(2)}, u32[]{:S(2)}) collective-permute-start(bf16[128,1792]{1,0:T(8,128)(2,1)S(1)} %gate.4), channel_id=1, source_target_pairs={{0,7},{1,6},{2,5},{3,4},{4,3},{5,2},{6,1},{7,0},{8,15},{9,14},{10,... | collective-permute-start | bytes 1376264 | tf_op jit(solution)/shard_map/ppermute | solution.py:233
  59.4 4.6 %collective-permute-done.11.refs_6_ = bf16[128,1792]{1,0:T(8,128)(2,1)S(1)} collective-permute-done((bf16[128,1792]{1,0:T(8,128)(2,1)S(1)}, bf16[128,1792]{1,0:T(8,128)(2,1)S(1)}, u32[]{:S(2)}, u32[]{:S(2)}) %collective-permute-start.11) | collective-permute-done | bytes 458784 | tf_op jit(solution)/shard_map/ppermute | solution.py:220
  64.0 0.0 collective-permute-start.9
  64.0 0.0 collective-permute-done.10.refs_5_
  64.0 0.5 collective-permute-start.12
  64.5 8.2 %collective-permute-done.14.refs_10_ = bf16[128,1792]{1,0:T(8,128)(2,1)S(1)} collective-permute-done((bf16[128,1792]{1,0:T(8,128)(2,1)S(1)}, bf16[128,1792]{1,0:T(8,128)(2,1)S(1)}, u32[]{:S(2)}, u32[]{:S(2)}) %collective-permute-start.14) | collective-permute-done | bytes 458784 | tf_op jit(solution)/shard_map/ppermute | solution.py:220
  72.7 0.0 collective-permute-start.15
  72.7 0.0 collective-permute-done.5.refs_6_
  72.7 1.3 %collective-permute-start.6 = (bf16[128,1792]{1,0:T(8,128)(2,1)S(1)}, bf16[128,1792]{1,0:T(8,128)(2,1)S(1)}, u32[]{:S(2)}, u32[]{:S(2)}) collective-permute-start(bf16[128,1792]{1,0:T(8,128)(2,1)S(1)} %gate.5), channel_id=1, source_target_pairs={{0,6},{1,7},{2,4},{3,5},{4,2},{5,3},{6,0},{7,1},{8,14},{9,15},{10,... | collective-permute-start | bytes 1376264 | tf_op jit(solution)/shard_map/ppermute | solution.py:233
  74.0 0.9 pack.11.refs_0_
  74.9 0.9 pack.6.refs_8_.refs_4_
  75.8 0.0 collective-permute-done.13.refs_9_
  75.8 1.6 %collective-permute-start.19 = (bf16[128,1792]{1,0:T(8,128)(2,1)S(1)}, bf16[128,1792]{1,0:T(8,128)(2,1)S(1)}, u32[]{:S(2)}, u32[]{:S(2)}) collective-permute-start(bf16[128,1792]{1,0:T(8,128)(2,1)S(1)} %pack.11.refs_0_), channel_id=1, source_target_pairs={{0,16},{8,24},{16,0},{24,8},{1,17},{9,25},{17,1},{25,9},{2,18},{10... | collective-permute-start | bytes 1376264 | tf_op jit(solution)/shard_map/ppermute | solution.py:220
  77.4 0.6 collective-permute-start.22
  78.0 4.6 %place.3 = (bf16[6,128,7168]{2,1,0:T(8,128)(2,1)}, f32[8,128]{1,0:T(8,128)S(1)}) custom-call(s32[24]{0:T(128)S(1)} %routing_table.1.table_ref, bf16[128,1792]{1,0:T(8,128)(2,1)S(1)} %pack.7.refs_0_, bf16[128,1792]{1,0:T(8,128)(2,1)S(1)} %collective-permute-done.7.refs_1_, bf16[128,1792]{1,0:T(8,128)(2,1)S(1)} %collective-permute-done.8.refs_2_, ...), custom_call_target="tpu_custom_call" | custom-call | bytes 22020096 | tf_op jit(solution)/shard_map/place/pallas_call | solution.py:173
  82.6 5.0 %collective-permute-done.6.refs_7_ = bf16[128,1792]{1,0:T(8,128)(2,1)S(1)} collective-permute-done((bf16[128,1792]{1,0:T(8,128)(2,1)S(1)}, bf16[128,1792]{1,0:T(8,128)(2,1)S(1)}, u32[]{:S(2)}, u32[]{:S(2)}) %collective-permute-start.6) | collective-permute-done | bytes 458784 | tf_op jit(solution)/shard_map/ppermute | solution.py:233
  87.6 0.9 pack.10.refs_8_
  88.5 1.5 %collective-permute-start.16 = (bf16[128,1792]{1,0:T(8,128)(2,1)S(1)}, bf16[128,1792]{1,0:T(8,128)(2,1)S(1)}, u32[]{:S(2)}, u32[]{:S(2)}) collective-permute-start(bf16[128,1792]{1,0:T(8,128)(2,1)S(1)} %pack.10.refs_8_), channel_id=1, source_target_pairs={{0,16},{8,24},{16,0},{24,8},{1,17},{9,25},{17,1},{25,9},{2,18},{10... | collective-permute-start | bytes 1376264 | tf_op jit(solution)/shard_map/ppermute | solution.py:220
  90.0 0.5 collective-permute-start.20
  90.5 8.6 %collective-permute-done.22.refs_6_ = bf16[128,1792]{1,0:T(8,128)(2,1)S(1)} collective-permute-done((bf16[128,1792]{1,0:T(8,128)(2,1)S(1)}, bf16[128,1792]{1,0:T(8,128)(2,1)S(1)}, u32[]{:S(2)}, u32[]{:S(2)}) %collective-permute-start.22) | collective-permute-done | bytes 458784 | tf_op jit(solution)/shard_map/ppermute | solution.py:220
  99.1 0.5 collective-permute-start.24
  99.6 8.6 %collective-permute-done.16.refs_0_ = bf16[128,1792]{1,0:T(8,128)(2,1)S(1)} collective-permute-done((bf16[128,1792]{1,0:T(8,128)(2,1)S(1)}, bf16[128,1792]{1,0:T(8,128)(2,1)S(1)}, u32[]{:S(2)}, u32[]{:S(2)}) %collective-permute-start.16) | collective-permute-done | bytes 458784 | tf_op jit(solution)/shard_map/ppermute | solution.py:220
  108.2 3.7 %place.4 = (bf16[6,128,7168]{2,1,0:T(8,128)(2,1)}, f32[8,128]{1,0:T(8,128)S(1)}) custom-call(s32[24]{0:T(128)S(1)} %routing_table.1.table_ref, bf16[128,1792]{1,0:T(8,128)(2,1)S(1)} %pack.11.refs_0_, bf16[128,1792]{1,0:T(8,128)(2,1)S(1)} %collective-permute-done.18.refs_1_, ...), custom_call_target="tpu_custom_call", output_to_operand_aliasing={{0}: (11, {})} | custom-call | bytes 18350080 | tf_op jit(solution)/shard_map/place/pallas_call | solution.py:173
  112.0 2.4 %place.5 = (bf16[6,128,7168]{2,1,0:T(8,128)(2,1)}, bf16[6,56]{1,0:T(8,128)(2,1)}) custom-call(s32[24]{0:T(128)S(1)} %routing_table.1.table_ref, bf16[128,1792]{1,0:T(8,128)(2,1)S(1)} %collective-permute-done.16.refs_0_, bf16[128,1792]{1,0:T(8,128)(2,1)S(1)} %collective-permute-done.17.refs_1_, ...), custom_call_target="tpu_custom_call", output_to_operand_aliasing={{0}: (3, {})} | custom-call | bytes 3670016 | tf_op jit(solution)/shard_map/place/pallas_call | solution.py:173
  (24 shorter events, 0.1 us)
Async XLA Ops:
  0.6 2.0 %copy-start = (bf16[8,128,1792]{2,1,0:T(8,128)(2,1)S(1)}, bf16[8,128,1792]{2,1,0:T(8,128)(2,1)}, u32[]{:S(2)}) copy-start(bf16[8,128,1792]{2,1,0:T(8,128)(2,1)} %w_ref.1) | copy-start | bytes 11010052
  2.7 0.7 copy-start.1
  6.6 13.6 %collective-permute-start = (bf16[128,1792]{1,0:T(8,128)(2,1)S(1)}, bf16[128,1792]{1,0:T(8,128)(2,1)S(1)}, u32[]{:S(2)}, u32[]{:S(2)}) collective-permute-start(bf16[128,1792]{1,0:T(8,128)(2,1)S(1)} %get-tuple-element.17), channel_id=1, source_target_pairs={{0,1},{1,0},{2,3},{3,2},{4,5},{5,4},{6,7},{7,6},{8,9},{9,8},{10,11... | collective-permute-start | bytes 1376264 | tf_op jit(solution)/shard_map/ppermute | solution.py:233
  9.6 32.9 %collective-permute-start.1 = (bf16[128,1792]{1,0:T(8,128)(2,1)S(1)}, bf16[128,1792]{1,0:T(8,128)(2,1)S(1)}, u32[]{:S(2)}, u32[]{:S(2)}) collective-permute-start(bf16[128,1792]{1,0:T(8,128)(2,1)S(1)} %get-tuple-element.18), channel_id=1, source_target_pairs={{0,2},{1,3},{2,0},{3,1},{4,6},{5,7},{6,4},{7,5},{8,10},{9,11},{10,... | collective-permute-start | bytes 1376264 | tf_op jit(solution)/shard_map/ppermute | solution.py:233
  11.2 38.5 %collective-permute-start.2 = (bf16[128,1792]{1,0:T(8,128)(2,1)S(1)}, bf16[128,1792]{1,0:T(8,128)(2,1)S(1)}, u32[]{:S(2)}, u32[]{:S(2)}) collective-permute-start(bf16[128,1792]{1,0:T(8,128)(2,1)S(1)} %get-tuple-element.19), channel_id=1, source_target_pairs={{0,3},{1,2},{2,1},{3,0},{4,7},{5,6},{6,5},{7,4},{8,11},{9,10},{10,... | collective-permute-start | bytes 1376264 | tf_op jit(solution)/shard_map/ppermute | solution.py:233
  11.2 41.0 %collective-permute-start.3 = (bf16[128,1792]{1,0:T(8,128)(2,1)S(1)}, bf16[128,1792]{1,0:T(8,128)(2,1)S(1)}, u32[]{:S(2)}, u32[]{:S(2)}) collective-permute-start(bf16[128,1792]{1,0:T(8,128)(2,1)S(1)} %get-tuple-element.20), channel_id=1, source_target_pairs={{0,4},{1,5},{2,6},{3,7},{4,0},{5,1},{6,2},{7,3},{8,12},{9,13},{10,... | collective-permute-start | bytes 1376264 | tf_op jit(solution)/shard_map/ppermute | solution.py:233
  14.2 0.7 copy-start.2
  14.8 0.7 copy-start.3
  20.1 34.3 %collective-permute-start.4 = (bf16[128,1792]{1,0:T(8,128)(2,1)S(1)}, bf16[128,1792]{1,0:T(8,128)(2,1)S(1)}, u32[]{:S(2)}, u32[]{:S(2)}) collective-permute-start(bf16[128,1792]{1,0:T(8,128)(2,1)S(1)} %gate.3), channel_id=1, source_target_pairs={{0,5},{1,4},{2,7},{3,6},{4,1},{5,0},{6,3},{7,2},{8,13},{9,12},{10,... | collective-permute-start | bytes 1376264 | tf_op jit(solution)/shard_map/ppermute | solution.py:233
  43.4 12.5 %collective-permute-start.8 = (bf16[128,1792]{1,0:T(8,128)(2,1)S(1)}, bf16[128,1792]{1,0:T(8,128)(2,1)S(1)}, u32[]{:S(2)}, u32[]{:S(2)}) collective-permute-start(bf16[128,1792]{1,0:T(8,128)(2,1)S(1)} %pack.7.refs_0_), channel_id=1, source_target_pairs={{0,16},{8,24},{16,0},{24,8},{1,17},{9,25},{17,1},{25,9},{2,18},{10... | collective-permute-start | bytes 1376264 | tf_op jit(solution)/shard_map/ppermute | solution.py:220
  44.9 14.5 %collective-permute-start.7 = (bf16[128,1792]{1,0:T(8,128)(2,1)S(1)}, bf16[128,1792]{1,0:T(8,128)(2,1)S(1)}, u32[]{:S(2)}, u32[]{:S(2)}) collective-permute-start(bf16[128,1792]{1,0:T(8,128)(2,1)S(1)} %pack.7.refs_0_), channel_id=1, source_target_pairs={{0,8},{8,0},{16,24},{24,16},{1,9},{9,1},{17,25},{25,17},{2,10},{10... | collective-permute-start | bytes 1376264 | tf_op jit(solution)/shard_map/ppermute | solution.py:220
  50.5 13.5 %collective-permute-start.11 = (bf16[128,1792]{1,0:T(8,128)(2,1)S(1)}, bf16[128,1792]{1,0:T(8,128)(2,1)S(1)}, u32[]{:S(2)}, u32[]{:S(2)}) collective-permute-start(bf16[128,1792]{1,0:T(8,128)(2,1)S(1)} %pack.8.refs_4_), channel_id=1, source_target_pairs={{0,16},{8,24},{16,0},{24,8},{1,17},{9,25},{17,1},{25,9},{2,18},{10... | collective-permute-start | bytes 1376264 | tf_op jit(solution)/shard_map/ppermute | solution.py:220
  52.2 11.8 %collective-permute-start.10 = (bf16[128,1792]{1,0:T(8,128)(2,1)S(1)}, bf16[128,1792]{1,0:T(8,128)(2,1)S(1)}, u32[]{:S(2)}, u32[]{:S(2)}) collective-permute-start(bf16[128,1792]{1,0:T(8,128)(2,1)S(1)} %pack.8.refs_4_), channel_id=1, source_target_pairs={{0,8},{8,0},{16,24},{24,16},{1,9},{9,1},{17,25},{25,17},{2,10},{10... | collective-permute-start | bytes 1376264 | tf_op jit(solution)/shard_map/ppermute | solution.py:220
  54.4 18.3 %collective-permute-start.14 = (bf16[128,1792]{1,0:T(8,128)(2,1)S(1)}, bf16[128,1792]{1,0:T(8,128)(2,1)S(1)}, u32[]{:S(2)}, u32[]{:S(2)}) collective-permute-start(bf16[128,1792]{1,0:T(8,128)(2,1)S(1)} %pack.9.refs_8_), channel_id=1, source_target_pairs={{0,16},{8,24},{16,0},{24,8},{1,17},{9,25},{17,1},{25,9},{2,18},{10... | collective-permute-start | bytes 1376264 | tf_op jit(solution)/shard_map/ppermute | solution.py:220
  55.9 16.8 %collective-permute-start.5 = (bf16[128,1792]{1,0:T(8,128)(2,1)S(1)}, bf16[128,1792]{1,0:T(8,128)(2,1)S(1)}, u32[]{:S(2)}, u32[]{:S(2)}) collective-permute-start(bf16[128,1792]{1,0:T(8,128)(2,1)S(1)} %gate.4), channel_id=1, source_target_pairs={{0,7},{1,6},{2,5},{3,4},{4,3},{5,2},{6,1},{7,0},{8,15},{9,14},{10,... | collective-permute-start | bytes 1376264 | tf_op jit(solution)/shard_map/ppermute | solution.py:233
  59.4 16.4 %collective-permute-start.13 = (bf16[128,1792]{1,0:T(8,128)(2,1)S(1)}, bf16[128,1792]{1,0:T(8,128)(2,1)S(1)}, u32[]{:S(2)}, u32[]{:S(2)}) collective-permute-start(bf16[128,1792]{1,0:T(8,128)(2,1)S(1)} %pack.9.refs_8_), channel_id=1, source_target_pairs={{0,8},{8,0},{16,24},{24,16},{1,9},{9,1},{17,25},{25,17},{2,10},{10... | collective-permute-start | bytes 1376264 | tf_op jit(solution)/shard_map/ppermute | solution.py:220
  64.0 13.3 %collective-permute-start.9 = (bf16[128,1792]{1,0:T(8,128)(2,1)S(1)}, bf16[128,1792]{1,0:T(8,128)(2,1)S(1)}, u32[]{:S(2)}, u32[]{:S(2)}) collective-permute-start(bf16[128,1792]{1,0:T(8,128)(2,1)S(1)} %collective-permute-done.8.refs_2_), channel_id=1, source_target_pairs={{0,8},{8,0},{16,24},{24,16},{1,9},{9,1},{17,25},{25,17},{2,10},{10... | collective-permute-start | bytes 1376264 | tf_op jit(solution)/shard_map/ppermute | solution.py:220
  64.0 13.3 %collective-permute-start.12 = (bf16[128,1792]{1,0:T(8,128)(2,1)S(1)}, bf16[128,1792]{1,0:T(8,128)(2,1)S(1)}, u32[]{:S(2)}, u32[]{:S(2)}) collective-permute-start(bf16[128,1792]{1,0:T(8,128)(2,1)S(1)} %collective-permute-done.11.refs_6_), channel_id=1, source_target_pairs={{0,8},{8,0},{16,24},{24,16},{1,9},{9,1},{17,25},{25,17},{2,10},{10... | collective-permute-start | bytes 1376264 | tf_op jit(solution)/shard_map/ppermute | solution.py:220
  72.7 5.3 %collective-permute-start.15 = (bf16[128,1792]{1,0:T(8,128)(2,1)S(1)}, bf16[128,1792]{1,0:T(8,128)(2,1)S(1)}, u32[]{:S(2)}, u32[]{:S(2)}) collective-permute-start(bf16[128,1792]{1,0:T(8,128)(2,1)S(1)} %collective-permute-done.14.refs_10_), channel_id=1, source_target_pairs={{0,8},{8,0},{16,24},{24,16},{1,9},{9,1},{17,25},{25,17},{2,10},{10... | collective-permute-start | bytes 1376264 | tf_op jit(solution)/shard_map/ppermute | solution.py:220
  72.7 14.8 %collective-permute-start.6 = (bf16[128,1792]{1,0:T(8,128)(2,1)S(1)}, bf16[128,1792]{1,0:T(8,128)(2,1)S(1)}, u32[]{:S(2)}, u32[]{:S(2)}) collective-permute-start(bf16[128,1792]{1,0:T(8,128)(2,1)S(1)} %gate.5), channel_id=1, source_target_pairs={{0,6},{1,7},{2,4},{3,5},{4,2},{5,3},{6,0},{7,1},{8,14},{9,15},{10,... | collective-permute-start | bytes 1376264 | tf_op jit(solution)/shard_map/ppermute | solution.py:233
  75.8 14.2 %collective-permute-start.19 = (bf16[128,1792]{1,0:T(8,128)(2,1)S(1)}, bf16[128,1792]{1,0:T(8,128)(2,1)S(1)}, u32[]{:S(2)}, u32[]{:S(2)}) collective-permute-start(bf16[128,1792]{1,0:T(8,128)(2,1)S(1)} %pack.11.refs_0_), channel_id=1, source_target_pairs={{0,16},{8,24},{16,0},{24,8},{1,17},{9,25},{17,1},{25,9},{2,18},{10... | collective-permute-start | bytes 1376264 | tf_op jit(solution)/shard_map/ppermute | solution.py:220
  77.4 21.7 %collective-permute-start.18 = (bf16[128,1792]{1,0:T(8,128)(2,1)S(1)}, bf16[128,1792]{1,0:T(8,128)(2,1)S(1)}, u32[]{:S(2)}, u32[]{:S(2)}) collective-permute-start(bf16[128,1792]{1,0:T(8,128)(2,1)S(1)} %pack.11.refs_0_), channel_id=1, source_target_pairs={{0,8},{8,0},{16,24},{24,16},{1,9},{9,1},{17,25},{25,17},{2,10},{10... | collective-permute-start | bytes 1376264 | tf_op jit(solution)/shard_map/ppermute | solution.py:220
  77.4 21.7 %collective-permute-start.22 = (bf16[128,1792]{1,0:T(8,128)(2,1)S(1)}, bf16[128,1792]{1,0:T(8,128)(2,1)S(1)}, u32[]{:S(2)}, u32[]{:S(2)}) collective-permute-start(bf16[128,1792]{1,0:T(8,128)(2,1)S(1)} %pack.6.refs_8_.refs_4_), channel_id=1, source_target_pairs={{0,16},{8,24},{16,0},{24,8},{1,17},{9,25},{17,1},{25,9},{2,18},{10... | collective-permute-start | bytes 1376264 | tf_op jit(solution)/shard_map/ppermute | solution.py:220
  88.5 19.7 %collective-permute-start.16 = (bf16[128,1792]{1,0:T(8,128)(2,1)S(1)}, bf16[128,1792]{1,0:T(8,128)(2,1)S(1)}, u32[]{:S(2)}, u32[]{:S(2)}) collective-permute-start(bf16[128,1792]{1,0:T(8,128)(2,1)S(1)} %pack.10.refs_8_), channel_id=1, source_target_pairs={{0,16},{8,24},{16,0},{24,8},{1,17},{9,25},{17,1},{25,9},{2,18},{10... | collective-permute-start | bytes 1376264 | tf_op jit(solution)/shard_map/ppermute | solution.py:220
  90.0 18.2 %collective-permute-start.21 = (bf16[128,1792]{1,0:T(8,128)(2,1)S(1)}, bf16[128,1792]{1,0:T(8,128)(2,1)S(1)}, u32[]{:S(2)}, u32[]{:S(2)}) collective-permute-start(bf16[128,1792]{1,0:T(8,128)(2,1)S(1)} %pack.6.refs_8_.refs_4_), channel_id=1, source_target_pairs={{0,8},{8,0},{16,24},{24,16},{1,9},{9,1},{17,25},{25,17},{2,10},{10... | collective-permute-start | bytes 1376264 | tf_op jit(solution)/shard_map/ppermute | solution.py:220
  90.0 18.2 %collective-permute-start.20 = (bf16[128,1792]{1,0:T(8,128)(2,1)S(1)}, bf16[128,1792]{1,0:T(8,128)(2,1)S(1)}, u32[]{:S(2)}, u32[]{:S(2)}) collective-permute-start(bf16[128,1792]{1,0:T(8,128)(2,1)S(1)} %collective-permute-done.19.refs_2_), channel_id=1, source_target_pairs={{0,8},{8,0},{16,24},{24,16},{1,9},{9,1},{17,25},{25,17},{2,10},{10... | collective-permute-start | bytes 1376264 | tf_op jit(solution)/shard_map/ppermute | solution.py:220
  99.1 9.1 %collective-permute-start.23 = (bf16[128,1792]{1,0:T(8,128)(2,1)S(1)}, bf16[128,1792]{1,0:T(8,128)(2,1)S(1)}, u32[]{:S(2)}, u32[]{:S(2)}) collective-permute-start(bf16[128,1792]{1,0:T(8,128)(2,1)S(1)} %collective-permute-done.22.refs_6_), channel_id=1, source_target_pairs={{0,8},{8,0},{16,24},{24,16},{1,9},{9,1},{17,25},{25,17},{2,10},{10... | collective-permute-start | bytes 1376264 | tf_op jit(solution)/shard_map/ppermute | solution.py:220
  99.1 9.1 %collective-permute-start.24 = (bf16[128,1792]{1,0:T(8,128)(2,1)S(1)}, bf16[128,1792]{1,0:T(8,128)(2,1)S(1)}, u32[]{:S(2)}, u32[]{:S(2)}) collective-permute-start(bf16[128,1792]{1,0:T(8,128)(2,1)S(1)} %pack.10.refs_8_), channel_id=1, source_target_pairs={{0,8},{8,0},{16,24},{24,16},{1,9},{9,1},{17,25},{25,17},{2,10},{10... | collective-permute-start | bytes 1376264 | tf_op jit(solution)/shard_map/ppermute | solution.py:220
  108.2 3.8 %collective-permute-start.17 = (bf16[128,1792]{1,0:T(8,128)(2,1)S(1)}, bf16[128,1792]{1,0:T(8,128)(2,1)S(1)}, u32[]{:S(2)}, u32[]{:S(2)}) collective-permute-start(bf16[128,1792]{1,0:T(8,128)(2,1)S(1)} %collective-permute-done.16.refs_0_), channel_id=1, source_target_pairs={{0,8},{8,0},{16,24},{24,16},{1,9},{9,1},{17,25},{25,17},{2,10},{10... | collective-permute-start | bytes 1376264 | tf_op jit(solution)/shard_map/ppermute | solution.py:220

commit v3 on v2

--- a/solution.py
+++ b/solution.py
@@ -17,6 +17,7 @@
 PICK, ROW, LIVE = 0, 8, 16
 VMEM_LIMIT = 8 * 1024 * 1024
 PLACE_LIMIT = 24 * 1024 * 1024
+PICK_LIMIT = 48 * 1024 * 1024
 
 ANY = pl.BlockSpec(memory_space=pl.ANY)
 HBM = pl.BlockSpec(memory_space=pltpu.HBM)
@@ -52,7 +53,7 @@
         in_specs=[SMEM, HBM],
         out_specs=[VMEM] * len(shifts),
         scratch_shapes=[pltpu.SemaphoreType.DMA((len(shifts),))],
-        compiler_params=pltpu.CompilerParams(vmem_limit_bytes=VMEM_LIMIT),
+        compiler_params=pltpu.CompilerParams(vmem_limit_bytes=PICK_LIMIT),
         name="pick",
     )(owner, weight)
 

time: 115 us -> 112 us (0.974)
  local copies, waits for them, and re-layouts: 4 us -> 1.96 us
    unnamed x8 -> x6, local copies, waits for them, and re-layouts: 4 us -> 1.96 us
where the time goes in v3:
time: 112 us; the launch traced here: 111 us
  waiting for transfers between devices  62.7 us (56%)
  starting transfers between devices  26.4 us (24%)
  Pallas kernels  19.4 us (17%)
  local copies, waits for them, and re-layouts  1.96 us (2%)
    ppermute x7, waiting for transfers between devices, arrival(): got[flip] = lax.ppermute(x, 'exp', pairs(owners, flip)) if flip else x  32.7 us
    ppermute x18, waiting for transfers between devices, over_rep(): return lax.ppermute(x, 'rep', pairs(replicas, flip))  30 us
    ppermute x7, starting transfers between devices, arrival(): got[flip] = lax.ppermute(x, 'exp', pairs(owners, flip)) if flip else x  16.5 us
    pallas_call x3, Pallas kernels, place(): pl.pallas_call(functools.partial(place_kernel, spots, fresh), out_shape=[...  10.2 us
    ppermute x18, starting transfers between devices, over_rep(): return lax.ppermute(x, 'rep', pairs(replicas, flip))  9.91 us
    pallas_call x6, Pallas kernels, pack(): pl.pallas_call(functools.partial(pack_kernel, j, len(arrived)), out_shape...  5.19 us
    pallas_call x1, Pallas kernels, pick(): pl.pallas_call(functools.partial(pick_kernel, shifts, local_count), out_s...  2.63 us
  transfers between devices with their start and end apart: 25, of which 9 were waited for; matrix products, arithmetic and copies ran while one was open for 0% of the time, Pallas kernels for 13%

profile of v3, /device:TPU:0, one launch (start us, length us, event | category | flops | bytes accessed | tf_op | source)
XLA Modules:
  0.0 111.2 jit_solution(195730426487500336)
XLA Ops:
  0.6 0.6 copy-done
  1.3 2.6 %pick.1 = (bf16[128,1792]{1,0:T(8,128)(2,1)S(1)}, bf16[128,1792]{1,0:T(8,128)(2,1)S(1)}, bf16[128,1792]{1,0:T(8,128)(2,1)S(1)}, bf16[128,1792]{1,0:T(8,128)(2,1)...) custom-call(s32[64]{0:T(128)S(1)} %copy-done, ...), custom_call_target="tpu_custom_call" | custom-call | tf_op jit(solution)/shard_map/pick/pallas_call | solution.py:50
  3.9 3.0 %collective-permute-start = (bf16[128,1792]{1,0:T(8,128)(2,1)S(1)}, bf16[128,1792]{1,0:T(8,128)(2,1)S(1)}, u32[]{:S(2)}, u32[]{:S(2)}) collective-permute-start(bf16[128,1792]{1,0:T(8,128)(2,1)S(1)} %get-tuple-element.17), channel_id=1, source_target_pairs={{0,1},{1,0},{2,3},{3,2},{4,5},{5,4},{6,7},{7,6},{8,9},{9,8},{10,11... | collective-permute-start | bytes 1376264 | tf_op jit(solution)/shard_map/ppermute | solution.py:234
  7.0 1.6 %collective-permute-start.1 = (bf16[128,1792]{1,0:T(8,128)(2,1)S(1)}, bf16[128,1792]{1,0:T(8,128)(2,1)S(1)}, u32[]{:S(2)}, u32[]{:S(2)}) collective-permute-start(bf16[128,1792]{1,0:T(8,128)(2,1)S(1)} %get-tuple-element.18), channel_id=1, source_target_pairs={{0,2},{1,3},{2,0},{3,1},{4,6},{5,7},{6,4},{7,5},{8,10},{9,11},{10,... | collective-permute-start | bytes 1376264 | tf_op jit(solution)/shard_map/ppermute | solution.py:234
  8.5 0.0 collective-permute-start.2
  8.5 3.0 %collective-permute-start.3 = (bf16[128,1792]{1,0:T(8,128)(2,1)S(1)}, bf16[128,1792]{1,0:T(8,128)(2,1)S(1)}, u32[]{:S(2)}, u32[]{:S(2)}) collective-permute-start(bf16[128,1792]{1,0:T(8,128)(2,1)S(1)} %get-tuple-element.20), channel_id=1, source_target_pairs={{0,4},{1,5},{2,6},{3,7},{4,0},{5,1},{6,2},{7,3},{8,12},{9,13},{10,... | collective-permute-start | bytes 1376264 | tf_op jit(solution)/shard_map/ppermute | solution.py:234
  11.5 0.7 copy-done.1
  12.2 0.7 copy-done.2
  12.8 1.4 %routing_table.1.table_ref = s32[24]{0:T(128)S(1)} custom-call(s32[64]{0:T(128)S(1)} %copy-done, s32[64]{0:T(128)S(1)} %copy-done.1, s32[64]{0:T(128)S(1)} %copy-done.2), custom_call_target="tpu_custom_call" | custom-call | tf_op jit(solution)/shard_map/routing_table/pallas_call | solution.py:88
  14.2 3.3 %collective-permute-done.refs_0_.refs_1_ = bf16[128,1792]{1,0:T(8,128)(2,1)S(1)} collective-permute-done((bf16[128,1792]{1,0:T(8,128)(2,1)S(1)}, bf16[128,1792]{1,0:T(8,128)(2,1)S(1)}, u32[]{:S(2)}, u32[]{:S(2)}) %collective-permute-start) | collective-permute-done | bytes 458784 | tf_op jit(solution)/shard_map/ppermute | solution.py:234
  17.5 4.0 %collective-permute-start.4 = (bf16[128,1792]{1,0:T(8,128)(2,1)S(1)}, bf16[128,1792]{1,0:T(8,128)(2,1)S(1)}, u32[]{:S(2)}, u32[]{:S(2)}) collective-permute-start(bf16[128,1792]{1,0:T(8,128)(2,1)S(1)} %gate.3), channel_id=1, source_target_pairs={{0,5},{1,4},{2,7},{3,6},{4,1},{5,0},{6,3},{7,2},{8,13},{9,12},{10,... | collective-permute-start | bytes 1376264 | tf_op jit(solution)/shard_map/ppermute | solution.py:234
  21.5 18.4 %collective-permute-done.1.refs_2_ = bf16[128,1792]{1,0:T(8,128)(2,1)S(1)} collective-permute-done((bf16[128,1792]{1,0:T(8,128)(2,1)S(1)}, bf16[128,1792]{1,0:T(8,128)(2,1)S(1)}, u32[]{:S(2)}, u32[]{:S(2)}) %collective-permute-start.1) | collective-permute-done | bytes 458784 | tf_op jit(solution)/shard_map/ppermute | solution.py:234
  39.9 0.8 pack.7.refs_0_
  40.7 1.5 %collective-permute-start.8 = (bf16[128,1792]{1,0:T(8,128)(2,1)S(1)}, bf16[128,1792]{1,0:T(8,128)(2,1)S(1)}, u32[]{:S(2)}, u32[]{:S(2)}) collective-permute-start(bf16[128,1792]{1,0:T(8,128)(2,1)S(1)} %pack.7.refs_0_), channel_id=1, source_target_pairs={{0,16},{8,24},{16,0},{24,8},{1,17},{9,25},{17,1},{25,9},{2,18},{10... | collective-permute-start | bytes 1376264 | tf_op jit(solution)/shard_map/ppermute | solution.py:221
  42.3 0.0 collective-permute-start.7
  42.3 4.7 %collective-permute-done.2.refs_0_.refs_3_ = bf16[128,1792]{1,0:T(8,128)(2,1)S(1)} collective-permute-done((bf16[128,1792]{1,0:T(8,128)(2,1)S(1)}, bf16[128,1792]{1,0:T(8,128)(2,1)S(1)}, u32[]{:S(2)}, u32[]{:S(2)}) %collective-permute-start.2) | collective-permute-done | bytes 458784 | tf_op jit(solution)/shard_map/ppermute | solution.py:234
  47.0 0.9 pack.8.refs_4_
  47.8 1.7 %collective-permute-start.11 = (bf16[128,1792]{1,0:T(8,128)(2,1)S(1)}, bf16[128,1792]{1,0:T(8,128)(2,1)S(1)}, u32[]{:S(2)}, u32[]{:S(2)}) collective-permute-start(bf16[128,1792]{1,0:T(8,128)(2,1)S(1)} %pack.8.refs_4_), channel_id=1, source_target_pairs={{0,16},{8,24},{16,0},{24,8},{1,17},{9,25},{17,1},{25,9},{2,18},{10... | collective-permute-start | bytes 1376264 | tf_op jit(solution)/shard_map/ppermute | solution.py:221
  49.6 0.0 collective-permute-done.3.refs_0_.refs_4_
  49.6 0.9 pack.9.refs_8_
  50.4 1.3 %collective-permute-done.4.refs_5_ = bf16[128,1792]{1,0:T(8,128)(2,1)S(1)} collective-permute-done((bf16[128,1792]{1,0:T(8,128)(2,1)S(1)}, bf16[128,1792]{1,0:T(8,128)(2,1)S(1)}, u32[]{:S(2)}, u32[]{:S(2)}) %collective-permute-start.4) | collective-permute-done | bytes 458784 | tf_op jit(solution)/shard_map/ppermute | solution.py:234
  51.7 1.5 %collective-permute-start.14 = (bf16[128,1792]{1,0:T(8,128)(2,1)S(1)}, bf16[128,1792]{1,0:T(8,128)(2,1)S(1)}, u32[]{:S(2)}, u32[]{:S(2)}) collective-permute-start(bf16[128,1792]{1,0:T(8,128)(2,1)S(1)} %pack.9.refs_8_), channel_id=1, source_target_pairs={{0,16},{8,24},{16,0},{24,8},{1,17},{9,25},{17,1},{25,9},{2,18},{10... | collective-permute-start | bytes 1376264 | tf_op jit(solution)/shard_map/ppermute | solution.py:221
  53.2 3.5 %collective-permute-start.5 = (bf16[128,1792]{1,0:T(8,128)(2,1)S(1)}, bf16[128,1792]{1,0:T(8,128)(2,1)S(1)}, u32[]{:S(2)}, u32[]{:S(2)}) collective-permute-start(bf16[128,1792]{1,0:T(8,128)(2,1)S(1)} %gate.4), channel_id=1, source_target_pairs={{0,7},{1,6},{2,5},{3,4},{4,3},{5,2},{6,1},{7,0},{8,15},{9,14},{10,... | collective-permute-start | bytes 1376264 | tf_op jit(solution)/shard_map/ppermute | solution.py:234
  56.8 4.6 %collective-permute-done.11.refs_6_ = bf16[128,1792]{1,0:T(8,128)(2,1)S(1)} collective-permute-done((bf16[128,1792]{1,0:T(8,128)(2,1)S(1)}, bf16[128,1792]{1,0:T(8,128)(2,1)S(1)}, u32[]{:S(2)}, u32[]{:S(2)}) %collective-permute-start.11) | collective-permute-done | bytes 458784 | tf_op jit(solution)/shard_map/ppermute | solution.py:221
  61.4 0.0 collective-permute-start.9
  61.4 0.0 collective-permute-done.10.refs_5_
  61.4 0.5 collective-permute-start.12
  61.9 8.2 %collective-permute-done.14.refs_10_ = bf16[128,1792]{1,0:T(8,128)(2,1)S(1)} collective-permute-done((bf16[128,1792]{1,0:T(8,128)(2,1)S(1)}, bf16[128,1792]{1,0:T(8,128)(2,1)S(1)}, u32[]{:S(2)}, u32[]{:S(2)}) %collective-permute-start.14) | collective-permute-done | bytes 458784 | tf_op jit(solution)/shard_map/ppermute | solution.py:221
  70.1 0.0 collective-permute-start.15
  70.1 1.3 %collective-permute-start.6 = (bf16[128,1792]{1,0:T(8,128)(2,1)S(1)}, bf16[128,1792]{1,0:T(8,128)(2,1)S(1)}, u32[]{:S(2)}, u32[]{:S(2)}) collective-permute-start(bf16[128,1792]{1,0:T(8,128)(2,1)S(1)} %gate.5), channel_id=1, source_target_pairs={{0,6},{1,7},{2,4},{3,5},{4,2},{5,3},{6,0},{7,1},{8,14},{9,15},{10,... | collective-permute-start | bytes 1376264 | tf_op jit(solution)/shard_map/ppermute | solution.py:234
  71.4 0.9 pack.11.refs_0_
  72.3 0.9 pack.6.refs_8_.refs_4_
  73.1 0.0 collective-permute-done.13.refs_9_
  73.2 1.6 %collective-permute-start.19 = (bf16[128,1792]{1,0:T(8,128)(2,1)S(1)}, bf16[128,1792]{1,0:T(8,128)(2,1)S(1)}, u32[]{:S(2)}, u32[]{:S(2)}) collective-permute-start(bf16[128,1792]{1,0:T(8,128)(2,1)S(1)} %pack.11.refs_0_), channel_id=1, source_target_pairs={{0,16},{8,24},{16,0},{24,8},{1,17},{9,25},{17,1},{25,9},{2,18},{10... | collective-permute-start | bytes 1376264 | tf_op jit(solution)/shard_map/ppermute | solution.py:221
  74.7 0.0 collective-permute-done.12.refs_7_
  74.7 0.6 collective-permute-start.22
  75.3 0.0 collective-permute-done.15.refs_11_
  75.3 4.6 %place.3 = (bf16[6,128,7168]{2,1,0:T(8,128)(2,1)}, f32[8,128]{1,0:T(8,128)S(1)}) custom-call(s32[24]{0:T(128)S(1)} %routing_table.1.table_ref, bf16[128,1792]{1,0:T(8,128)(2,1)S(1)} %pack.7.refs_0_, bf16[128,1792]{1,0:T(8,128)(2,1)S(1)} %collective-permute-done.7.refs_1_, bf16[128,1792]{1,0:T(8,128)(2,1)S(1)} %collective-permute-done.8.refs_2_, ...), custom_call_target="tpu_custom_call" | custom-call | bytes 22020096 | tf_op jit(solution)/shard_map/place/pallas_call | solution.py:174
  79.9 5.0 %collective-permute-done.6.refs_7_ = bf16[128,1792]{1,0:T(8,128)(2,1)S(1)} collective-permute-done((bf16[128,1792]{1,0:T(8,128)(2,1)S(1)}, bf16[128,1792]{1,0:T(8,128)(2,1)S(1)}, u32[]{:S(2)}, u32[]{:S(2)}) %collective-permute-start.6) | collective-permute-done | bytes 458784 | tf_op jit(solution)/shard_map/ppermute | solution.py:234
  84.9 0.9 pack.10.refs_8_
  85.8 1.5 %collective-permute-start.16 = (bf16[128,1792]{1,0:T(8,128)(2,1)S(1)}, bf16[128,1792]{1,0:T(8,128)(2,1)S(1)}, u32[]{:S(2)}, u32[]{:S(2)}) collective-permute-start(bf16[128,1792]{1,0:T(8,128)(2,1)S(1)} %pack.10.refs_8_), channel_id=1, source_target_pairs={{0,16},{8,24},{16,0},{24,8},{1,17},{9,25},{17,1},{25,9},{2,18},{10... | collective-permute-start | bytes 1376264 | tf_op jit(solution)/shard_map/ppermute | solution.py:221
  87.3 0.0 collective-permute-start.21
  87.3 0.5 collective-permute-start.20
  87.8 8.6 %collective-permute-done.22.refs_6_ = bf16[128,1792]{1,0:T(8,128)(2,1)S(1)} collective-permute-done((bf16[128,1792]{1,0:T(8,128)(2,1)S(1)}, bf16[128,1792]{1,0:T(8,128)(2,1)S(1)}, u32[]{:S(2)}, u32[]{:S(2)}) %collective-permute-start.22) | collective-permute-done | bytes 458784 | tf_op jit(solution)/shard_map/ppermute | solution.py:221
  96.4 0.5 collective-permute-start.24
  96.9 8.6 %collective-permute-done.16.refs_0_ = bf16[128,1792]{1,0:T(8,128)(2,1)S(1)} collective-permute-done((bf16[128,1792]{1,0:T(8,128)(2,1)S(1)}, bf16[128,1792]{1,0:T(8,128)(2,1)S(1)}, u32[]{:S(2)}, u32[]{:S(2)}) %collective-permute-start.16) | collective-permute-done | bytes 458784 | tf_op jit(solution)/shard_map/ppermute | solution.py:221
  105.6 3.3 %place.4 = (bf16[6,128,7168]{2,1,0:T(8,128)(2,1)}, f32[8,128]{1,0:T(8,128)S(1)}) custom-call(s32[24]{0:T(128)S(1)} %routing_table.1.table_ref, bf16[128,1792]{1,0:T(8,128)(2,1)S(1)} %pack.11.refs_0_, bf16[128,1792]{1,0:T(8,128)(2,1)S(1)} %collective-permute-done.18.refs_1_, ...), custom_call_target="tpu_custom_call", output_to_operand_aliasing={{0}: (11, {})} | custom-call | bytes 18350080 | tf_op jit(solution)/shard_map/place/pallas_call | solution.py:174
  108.8 2.4 %place.5 = (bf16[6,128,7168]{2,1,0:T(8,128)(2,1)}, bf16[6,56]{1,0:T(8,128)(2,1)}) custom-call(s32[24]{0:T(128)S(1)} %routing_table.1.table_ref, bf16[128,1792]{1,0:T(8,128)(2,1)S(1)} %collective-permute-done.16.refs_0_, bf16[128,1792]{1,0:T(8,128)(2,1)S(1)} %collective-permute-done.17.refs_1_, ...), custom_call_target="tpu_custom_call", output_to_operand_aliasing={{0}: (3, {})} | custom-call | bytes 3670016 | tf_op jit(solution)/shard_map/place/pallas_call | solution.py:174
  (22 shorter events, 0.0 us)
Async XLA Ops:
  0.6 0.7 copy-start
  3.9 13.6 %collective-permute-start = (bf16[128,1792]{1,0:T(8,128)(2,1)S(1)}, bf16[128,1792]{1,0:T(8,128)(2,1)S(1)}, u32[]{:S(2)}, u32[]{:S(2)}) collective-permute-start(bf16[128,1792]{1,0:T(8,128)(2,1)S(1)} %get-tuple-element.17), channel_id=1, source_target_pairs={{0,1},{1,0},{2,3},{3,2},{4,5},{5,4},{6,7},{7,6},{8,9},{9,8},{10,11... | collective-permute-start | bytes 1376264 | tf_op jit(solution)/shard_map/ppermute | solution.py:234
  7.0 32.9 %collective-permute-start.1 = (bf16[128,1792]{1,0:T(8,128)(2,1)S(1)}, bf16[128,1792]{1,0:T(8,128)(2,1)S(1)}, u32[]{:S(2)}, u32[]{:S(2)}) collective-permute-start(bf16[128,1792]{1,0:T(8,128)(2,1)S(1)} %get-tuple-element.18), channel_id=1, source_target_pairs={{0,2},{1,3},{2,0},{3,1},{4,6},{5,7},{6,4},{7,5},{8,10},{9,11},{10,... | collective-permute-start | bytes 1376264 | tf_op jit(solution)/shard_map/ppermute | solution.py:234
  8.5 38.5 %collective-permute-start.2 = (bf16[128,1792]{1,0:T(8,128)(2,1)S(1)}, bf16[128,1792]{1,0:T(8,128)(2,1)S(1)}, u32[]{:S(2)}, u32[]{:S(2)}) collective-permute-start(bf16[128,1792]{1,0:T(8,128)(2,1)S(1)} %get-tuple-element.19), channel_id=1, source_target_pairs={{0,3},{1,2},{2,1},{3,0},{4,7},{5,6},{6,5},{7,4},{8,11},{9,10},{10,... | collective-permute-start | bytes 1376264 | tf_op jit(solution)/shard_map/ppermute | solution.py:234
  8.5 41.0 %collective-permute-start.3 = (bf16[128,1792]{1,0:T(8,128)(2,1)S(1)}, bf16[128,1792]{1,0:T(8,128)(2,1)S(1)}, u32[]{:S(2)}, u32[]{:S(2)}) collective-permute-start(bf16[128,1792]{1,0:T(8,128)(2,1)S(1)} %get-tuple-element.20), channel_id=1, source_target_pairs={{0,4},{1,5},{2,6},{3,7},{4,0},{5,1},{6,2},{7,3},{8,12},{9,13},{10,... | collective-permute-start | bytes 1376264 | tf_op jit(solution)/shard_map/ppermute | solution.py:234
  11.5 0.7 copy-start.1
  12.2 0.7 copy-start.2
  17.5 34.3 %collective-permute-start.4 = (bf16[128,1792]{1,0:T(8,128)(2,1)S(1)}, bf16[128,1792]{1,0:T(8,128)(2,1)S(1)}, u32[]{:S(2)}, u32[]{:S(2)}) collective-permute-start(bf16[128,1792]{1,0:T(8,128)(2,1)S(1)} %gate.3), channel_id=1, source_target_pairs={{0,5},{1,4},{2,7},{3,6},{4,1},{5,0},{6,3},{7,2},{8,13},{9,12},{10,... | collective-permute-start | bytes 1376264 | tf_op jit(solution)/shard_map/ppermute | solution.py:234
  40.7 12.5 %collective-permute-start.8 = (bf16[128,1792]{1,0:T(8,128)(2,1)S(1)}, bf16[128,1792]{1,0:T(8,128)(2,1)S(1)}, u32[]{:S(2)}, u32[]{:S(2)}) collective-permute-start(bf16[128,1792]{1,0:T(8,128)(2,1)S(1)} %pack.7.refs_0_), channel_id=1, source_target_pairs={{0,16},{8,24},{16,0},{24,8},{1,17},{9,25},{17,1},{25,9},{2,18},{10... | collective-permute-start | bytes 1376264 | tf_op jit(solution)/shard_map/ppermute | solution.py:221
  42.3 14.5 %collective-permute-start.7 = (bf16[128,1792]{1,0:T(8,128)(2,1)S(1)}, bf16[128,1792]{1,0:T(8,128)(2,1)S(1)}, u32[]{:S(2)}, u32[]{:S(2)}) collective-permute-start(bf16[128,1792]{1,0:T(8,128)(2,1)S(1)} %pack.7.refs_0_), channel_id=1, source_target_pairs={{0,8},{8,0},{16,24},{24,16},{1,9},{9,1},{17,25},{25,17},{2,10},{10... | collective-permute-start | bytes 1376264 | tf_op jit(solution)/shard_map/ppermute | solution.py:221
  47.8 13.5 %collective-permute-start.11 = (bf16[128,1792]{1,0:T(8,128)(2,1)S(1)}, bf16[128,1792]{1,0:T(8,128)(2,1)S(1)}, u32[]{:S(2)}, u32[]{:S(2)}) collective-permute-start(bf16[128,1792]{1,0:T(8,128)(2,1)S(1)} %pack.8.refs_4_), channel_id=1, source_target_pairs={{0,16},{8,24},{16,0},{24,8},{1,17},{9,25},{17,1},{25,9},{2,18},{10... | collective-permute-start | bytes 1376264 | tf_op jit(solution)/shard_map/ppermute | solution.py:221
  49.6 11.8 %collective-permute-start.10 = (bf16[128,1792]{1,0:T(8,128)(2,1)S(1)}, bf16[128,1792]{1,0:T(8,128)(2,1)S(1)}, u32[]{:S(2)}, u32[]{:S(2)}) collective-permute-start(bf16[128,1792]{1,0:T(8,128)(2,1)S(1)} %pack.8.refs_4_), channel_id=1, source_target_pairs={{0,8},{8,0},{16,24},{24,16},{1,9},{9,1},{17,25},{25,17},{2,10},{10... | collective-permute-start | bytes 1376264 | tf_op jit(solution)/shard_map/ppermute | solution.py:221
  51.7 18.3 %collective-permute-start.14 = (bf16[128,1792]{1,0:T(8,128)(2,1)S(1)}, bf16[128,1792]{1,0:T(8,128)(2,1)S(1)}, u32[]{:S(2)}, u32[]{:S(2)}) collective-permute-start(bf16[128,1792]{1,0:T(8,128)(2,1)S(1)} %pack.9.refs_8_), channel_id=1, source_target_pairs={{0,16},{8,24},{16,0},{24,8},{1,17},{9,25},{17,1},{25,9},{2,18},{10... | collective-permute-start | bytes 1376264 | tf_op jit(solution)/shard_map/ppermute | solution.py:221
  53.2 16.8 %collective-permute-start.5 = (bf16[128,1792]{1,0:T(8,128)(2,1)S(1)}, bf16[128,1792]{1,0:T(8,128)(2,1)S(1)}, u32[]{:S(2)}, u32[]{:S(2)}) collective-permute-start(bf16[128,1792]{1,0:T(8,128)(2,1)S(1)} %gate.4), channel_id=1, source_target_pairs={{0,7},{1,6},{2,5},{3,4},{4,3},{5,2},{6,1},{7,0},{8,15},{9,14},{10,... | collective-permute-start | bytes 1376264 | tf_op jit(solution)/shard_map/ppermute | solution.py:234
  56.8 16.4 %collective-permute-start.13 = (bf16[128,1792]{1,0:T(8,128)(2,1)S(1)}, bf16[128,1792]{1,0:T(8,128)(2,1)S(1)}, u32[]{:S(2)}, u32[]{:S(2)}) collective-permute-start(bf16[128,1792]{1,0:T(8,128)(2,1)S(1)} %pack.9.refs_8_), channel_id=1, source_target_pairs={{0,8},{8,0},{16,24},{24,16},{1,9},{9,1},{17,25},{25,17},{2,10},{10... | collective-permute-start | bytes 1376264 | tf_op jit(solution)/shard_map/ppermute | solution.py:221
  61.4 13.3 %collective-permute-start.9 = (bf16[128,1792]{1,0:T(8,128)(2,1)S(1)}, bf16[128,1792]{1,0:T(8,128)(2,1)S(1)}, u32[]{:S(2)}, u32[]{:S(2)}) collective-permute-start(bf16[128,1792]{1,0:T(8,128)(2,1)S(1)} %collective-permute-done.8.refs_2_), channel_id=1, source_target_pairs={{0,8},{8,0},{16,24},{24,16},{1,9},{9,1},{17,25},{25,17},{2,10},{10... | collective-permute-start | bytes 1376264 | tf_op jit(solution)/shard_map/ppermute | solution.py:221
  61.4 13.3 %collective-permute-start.12 = (bf16[128,1792]{1,0:T(8,128)(2,1)S(1)}, bf16[128,1792]{1,0:T(8,128)(2,1)S(1)}, u32[]{:S(2)}, u32[]{:S(2)}) collective-permute-start(bf16[128,1792]{1,0:T(8,128)(2,1)S(1)} %collective-permute-done.11.refs_6_), channel_id=1, source_target_pairs={{0,8},{8,0},{16,24},{24,16},{1,9},{9,1},{17,25},{25,17},{2,10},{10... | collective-permute-start | bytes 1376264 | tf_op jit(solution)/shard_map/ppermute | solution.py:221
  70.1 5.3 %collective-permute-start.15 = (bf16[128,1792]{1,0:T(8,128)(2,1)S(1)}, bf16[128,1792]{1,0:T(8,128)(2,1)S(1)}, u32[]{:S(2)}, u32[]{:S(2)}) collective-permute-start(bf16[128,1792]{1,0:T(8,128)(2,1)S(1)} %collective-permute-done.14.refs_10_), channel_id=1, source_target_pairs={{0,8},{8,0},{16,24},{24,16},{1,9},{9,1},{17,25},{25,17},{2,10},{10... | collective-permute-start | bytes 1376264 | tf_op jit(solution)/shard_map/ppermute | solution.py:221
  70.1 14.8 %collective-permute-start.6 = (bf16[128,1792]{1,0:T(8,128)(2,1)S(1)}, bf16[128,1792]{1,0:T(8,128)(2,1)S(1)}, u32[]{:S(2)}, u32[]{:S(2)}) collective-permute-start(bf16[128,1792]{1,0:T(8,128)(2,1)S(1)} %gate.5), channel_id=1, source_target_pairs={{0,6},{1,7},{2,4},{3,5},{4,2},{5,3},{6,0},{7,1},{8,14},{9,15},{10,... | collective-permute-start | bytes 1376264 | tf_op jit(solution)/shard_map/ppermute | solution.py:234
  73.2 14.2 %collective-permute-start.19 = (bf16[128,1792]{1,0:T(8,128)(2,1)S(1)}, bf16[128,1792]{1,0:T(8,128)(2,1)S(1)}, u32[]{:S(2)}, u32[]{:S(2)}) collective-permute-start(bf16[128,1792]{1,0:T(8,128)(2,1)S(1)} %pack.11.refs_0_), channel_id=1, source_target_pairs={{0,16},{8,24},{16,0},{24,8},{1,17},{9,25},{17,1},{25,9},{2,18},{10... | collective-permute-start | bytes 1376264 | tf_op jit(solution)/shard_map/ppermute | solution.py:221
  74.7 21.7 %collective-permute-start.18 = (bf16[128,1792]{1,0:T(8,128)(2,1)S(1)}, bf16[128,1792]{1,0:T(8,128)(2,1)S(1)}, u32[]{:S(2)}, u32[]{:S(2)}) collective-permute-start(bf16[128,1792]{1,0:T(8,128)(2,1)S(1)} %pack.11.refs_0_), channel_id=1, source_target_pairs={{0,8},{8,0},{16,24},{24,16},{1,9},{9,1},{17,25},{25,17},{2,10},{10... | collective-permute-start | bytes 1376264 | tf_op jit(solution)/shard_map/ppermute | solution.py:221
  74.7 21.7 %collective-permute-start.22 = (bf16[128,1792]{1,0:T(8,128)(2,1)S(1)}, bf16[128,1792]{1,0:T(8,128)(2,1)S(1)}, u32[]{:S(2)}, u32[]{:S(2)}) collective-permute-start(bf16[128,1792]{1,0:T(8,128)(2,1)S(1)} %pack.6.refs_8_.refs_4_), channel_id=1, source_target_pairs={{0,16},{8,24},{16,0},{24,8},{1,17},{9,25},{17,1},{25,9},{2,18},{10... | collective-permute-start | bytes 1376264 | tf_op jit(solution)/shard_map/ppermute | solution.py:221
  85.8 19.7 %collective-permute-start.16 = (bf16[128,1792]{1,0:T(8,128)(2,1)S(1)}, bf16[128,1792]{1,0:T(8,128)(2,1)S(1)}, u32[]{:S(2)}, u32[]{:S(2)}) collective-permute-start(bf16[128,1792]{1,0:T(8,128)(2,1)S(1)} %pack.10.refs_8_), channel_id=1, source_target_pairs={{0,16},{8,24},{16,0},{24,8},{1,17},{9,25},{17,1},{25,9},{2,18},{10... | collective-permute-start | bytes 1376264 | tf_op jit(solution)/shard_map/ppermute | solution.py:221
  87.3 18.2 %collective-permute-start.21 = (bf16[128,1792]{1,0:T(8,128)(2,1)S(1)}, bf16[128,1792]{1,0:T(8,128)(2,1)S(1)}, u32[]{:S(2)}, u32[]{:S(2)}) collective-permute-start(bf16[128,1792]{1,0:T(8,128)(2,1)S(1)} %pack.6.refs_8_.refs_4_), channel_id=1, source_target_pairs={{0,8},{8,0},{16,24},{24,16},{1,9},{9,1},{17,25},{25,17},{2,10},{10... | collective-permute-start | bytes 1376264 | tf_op jit(solution)/shard_map/ppermute | solution.py:221
  87.3 18.2 %collective-permute-start.20 = (bf16[128,1792]{1,0:T(8,128)(2,1)S(1)}, bf16[128,1792]{1,0:T(8,128)(2,1)S(1)}, u32[]{:S(2)}, u32[]{:S(2)}) collective-permute-start(bf16[128,1792]{1,0:T(8,128)(2,1)S(1)} %collective-permute-done.19.refs_2_), channel_id=1, source_target_pairs={{0,8},{8,0},{16,24},{24,16},{1,9},{9,1},{17,25},{25,17},{2,10},{10... | collective-permute-start | bytes 1376264 | tf_op jit(solution)/shard_map/ppermute | solution.py:221
  96.4 9.1 %collective-permute-start.23 = (bf16[128,1792]{1,0:T(8,128)(2,1)S(1)}, bf16[128,1792]{1,0:T(8,128)(2,1)S(1)}, u32[]{:S(2)}, u32[]{:S(2)}) collective-permute-start(bf16[128,1792]{1,0:T(8,128)(2,1)S(1)} %collective-permute-done.22.refs_6_), channel_id=1, source_target_pairs={{0,8},{8,0},{16,24},{24,16},{1,9},{9,1},{17,25},{25,17},{2,10},{10... | collective-permute-start | bytes 1376264 | tf_op jit(solution)/shard_map/ppermute | solution.py:221
  96.4 9.1 %collective-permute-start.24 = (bf16[128,1792]{1,0:T(8,128)(2,1)S(1)}, bf16[128,1792]{1,0:T(8,128)(2,1)S(1)}, u32[]{:S(2)}, u32[]{:S(2)}) collective-permute-start(bf16[128,1792]{1,0:T(8,128)(2,1)S(1)} %pack.10.refs_8_), channel_id=1, source_target_pairs={{0,8},{8,0},{16,24},{24,16},{1,9},{9,1},{17,25},{25,17},{2,10},{10... | collective-permute-start | bytes 1376264 | tf_op jit(solution)/shard_map/ppermute | solution.py:221
  105.5 3.3 %collective-permute-start.17 = (bf16[128,1792]{1,0:T(8,128)(2,1)S(1)}, bf16[128,1792]{1,0:T(8,128)(2,1)S(1)}, u32[]{:S(2)}, u32[]{:S(2)}) collective-permute-start(bf16[128,1792]{1,0:T(8,128)(2,1)S(1)} %collective-permute-done.16.refs_0_), channel_id=1, source_target_pairs={{0,8},{8,0},{16,24},{24,16},{1,9},{9,1},{17,25},{25,17},{2,10},{10... | collective-permute-start | bytes 1376264 | tf_op jit(solution)/shard_map/ppermute | solution.py:221
